TPU v7x, 32 devices: a whole 2x2x4 slice. The times are simulated.
32 devices in a mesh: chain: 8 (over y, x, core), tp: 4 (over z).
Axes of the slice: x: 2, y: 2, z: 4, core: 2. Of those that a mesh axis runs over, the one named last changes fastest.
Arguments:
- tokens: bfloat16 [4096, 8192], P('chain', 'tp'), may hold values from -800 to 800
- gain: float32 [8192], replicated, may hold values from 0.6 to 5
- w_query: bfloat16 [8192, 8192], P(None, 'tp'), may hold values from -0.125 to 0.125
- key_value_weight: bfloat16 [8192, 2048], P(None, 'tp'), may hold values from -0.125 to 0.125
- offsets: int32 [8], P('chain'), may hold values from 0 to 4032, as said below
- lengths: int32 [4], replicated, may hold values from 1 to 4096, as said below
Outputs:
- context: bfloat16 [4096, 8192], P('chain', 'tp')
- decode_cache: bfloat16 [16384, 2048], P('chain', 'tp')
Inputs may be any that keep to these rules, and one draw needn't show every extreme that they name: `offsets`: the first stretch starts at position 0, each later stretch starts at least 512 positions after the previous one, and the last one starts at (8 - 1) * 576. `lengths`: some decode group receives all 4096 tokens.
All inputs are finite; a program needn't handle non-finite values.
Results may differ from a plain program's by a relative error of at most 0.012.
The roundings to bfloat16 on the way count: a program that leaves them out, or rounds other values in their place, can miss the bound.
Values may be sent and summed in bfloat16 or wider, within the bound.
No kernel may reach another device: no remote copies, remote signals or barrier semaphores. Data moves between devices by JAX's collectives and lax.ppermute only.
A program may use at most 320 MiB of HBM per device.

v0:
```python
import jax
import jax.numpy as jnp
from jax import lax
from jax.sharding import PartitionSpec as P

HEAD_SIZE = 128
GROUPS = 4


def passed_along(x, axis, by):
    length = lax.axis_size(axis)
    return lax.ppermute(x, axis, [(i, (i + by) % length) for i in range(length)])


def rotary(vec, pos):
    half = vec.shape[-1] // 2
    freq = jnp.power(
        jnp.float32(500000.0), -2.0 * jnp.arange(half).astype(jnp.float32) / vec.shape[-1]
    )
    angle = pos.astype(jnp.float32)[:, None] * freq[None, :]
    cosine = jnp.cos(angle)[:, None, :]
    sine = jnp.sin(angle)[:, None, :]
    first = vec[..., :half]
    second = vec[..., half:]
    return jnp.concatenate(
        [first * cosine - second * sine, second * cosine + first * sine], axis=-1
    )


def attend(state, query_set, query_index, block, key_start, kv_local, head_dim):
    count = block.shape[0]
    scale = jnp.float32(1.0 / head_dim**0.5)
    needed = (key_start <= jnp.max(query_index)) & (key_start + count > 0)

    def run(inner):
        running, total, accum = inner
        parts = block.reshape(count, kv_local, 2, head_dim)
        kblock = parts[:, :, 0]
        vblock = parts[:, :, 1]
        key_index = key_start + jnp.arange(count, dtype=jnp.int32)
        valid = (key_index[None, :] <= query_index[:, None]) & (key_index[None, :] >= 0)
        scores = (
            jnp.einsum("chgd,nhd->hgcn", query_set, kblock, preferred_element_type=jnp.float32)
            * scale
        )
        scores = jnp.where(valid[None, None], scores, jnp.float32(-1e30))
        updated = jnp.maximum(running, jnp.max(scores, axis=-1))
        prob = jnp.where(valid[None, None], jnp.exp(scores - updated[..., None]), jnp.float32(0.0))
        factor = jnp.exp(running - updated)
        total = total * factor + jnp.sum(prob, axis=-1)
        weights = prob.astype(jnp.bfloat16)
        accum = accum * factor[..., None] + jnp.einsum(
            "hgcn,nhd->hgcd", weights, vblock, preferred_element_type=jnp.float32
        )
        return (updated, total, accum)

    def keep(inner):
        return inner

    return lax.cond(needed, run, keep, state)


def finish(state, count, q_local, head_dim):
    _, total, accum = state
    heads = accum / total[..., None]
    return (
        jnp.transpose(heads, (2, 0, 1, 3)).reshape(count, q_local * head_dim).astype(jnp.bfloat16)
    )


def local(tokens, gain, w_query, key_value_weight, offsets, lengths):
    rows = tokens.shape[0]
    head_dim = HEAD_SIZE
    kv_local = key_value_weight.shape[1] // (2 * head_dim)
    q_local = w_query.shape[1] // head_dim
    query_group_ratio = q_local // kv_local
    chain_pos = lax.axis_index("chain")
    chain_len = lax.axis_size("chain")
    whole = lax.all_gather(tokens, "tp", axis=1, tiled=True)
    wf = whole.astype(jnp.float32)
    inv_rms = lax.rsqrt(jnp.mean(wf * wf, axis=1) + 1e-05)
    normed = (wf * gain[None, :]).astype(jnp.bfloat16)
    query = jnp.dot(normed, w_query, preferred_element_type=jnp.float32)
    key_value_pair = jnp.dot(normed, key_value_weight, preferred_element_type=jnp.float32)
    query = query * inv_rms[:, None]
    key_value_pair = key_value_pair * inv_rms[:, None]
    position = offsets[0] + jnp.arange(rows, dtype=jnp.int32)
    rquery = rotary(query.reshape(rows, q_local, head_dim), position).astype(jnp.bfloat16)
    rquery = rquery.reshape(rows, kv_local, query_group_ratio, head_dim)
    key_value_pair = key_value_pair.reshape(rows, kv_local, 2, head_dim)
    rotated_keys = rotary(key_value_pair[:, :, 0], position).astype(jnp.bfloat16)
    value_rows = key_value_pair[:, :, 1].astype(jnp.bfloat16)
    key_value_row = jnp.stack([rotated_keys, value_rows], axis=2).reshape(
        rows, kv_local * 2 * head_dim
    )
    query_sets = (rquery,)
    query_indices = (chain_pos * rows + jnp.arange(rows, dtype=jnp.int32),)

    def attend_sets(states, block, key_start):
        return tuple(
            (
                attend(
                    states[k], query_sets[k], query_indices[k], block, key_start, kv_local, head_dim
                )
                for k in range(len(query_sets))
            )
        )

    init = tuple(
        (
            (
                jnp.full((kv_local, query_group_ratio, qs.shape[0]), -1e30, jnp.float32),
                jnp.zeros((kv_local, query_group_ratio, qs.shape[0]), jnp.float32),
                jnp.zeros((kv_local, query_group_ratio, qs.shape[0], head_dim), jnp.float32),
            )
            for qs in query_sets
        )
    )
    cache_rows = GROUPS * rows
    members = chain_len // GROUPS
    group_id = chain_pos // members
    first_span = chain_pos % members * GROUPS
    cache_first = first_span * rows
    empty = jnp.zeros((cache_rows, key_value_row.shape[1]), jnp.bfloat16)

    def place(handed_now, buffer, source):
        relative = source - first_span
        owned = (relative >= 0) & (relative < GROUPS)
        where_at = jnp.clip(relative, 0, GROUPS - 1) * rows
        updated = lax.dynamic_update_slice_in_dim(handed_now, buffer, where_at, 0)
        return jnp.where(owned, updated, handed_now)

    states = attend_sets(init, key_value_row, chain_pos * rows)
    handed = place(empty, key_value_row, chain_pos)

    def step_once(turn, carry):
        buffer, inner, handed_now = carry
        buffer = passed_along(buffer, "chain", 1)
        source = (chain_pos - turn + chain_len) % chain_len
        inner = attend_sets(inner, buffer, source * rows)
        handed_now = place(handed_now, buffer, source)
        return (buffer, inner, handed_now)

    _, states, handed = lax.fori_loop(1, chain_len, step_once, (key_value_row, states, handed))
    context = finish(states[0], rows, q_local, head_dim)
    group_length = jnp.sum(jnp.where(jnp.arange(GROUPS) == group_id, lengths, 0))
    token_index = cache_first + jnp.arange(cache_rows, dtype=jnp.int32)
    decode_cache = jnp.where((token_index < group_length)[:, None], handed, jnp.zeros_like(handed))
    return (context, decode_cache)


def solution(mesh):
    in_specs = (P("chain", "tp"), P(), P(None, "tp"), P(None, "tp"), P("chain"), P())
    out_specs = (P("chain", "tp"), P("chain", "tp"))
    return jax.shard_map(local, mesh=mesh, in_specs=in_specs, out_specs=out_specs, check_vma=False)
```

profile of v0, /device:TPU:15, one launch (start us, length us, event | category | flops | bytes accessed | tf_op | source)
XLA Modules:
  0.0 456.8 jit_solution(2289071073360349473)
XLA Ops:
  13.3 144.3 %all-gather.2.cloned.1.call-done = bf16[512,8192]{1,0:T(8,128)(2,1)} async-done(((bf16[512,2048]{1,0:T(8,128)(2,1)}), bf16[512,8192]{1,0:T(8,128)(2,1)}) %all-gather.2.cloned.1.call-update) | async-done | bytes 8388624 | tf_op jit(solution)/shard_map/all_gather | solution.py:79
  162.7 9.7 %fusion.39 = f32[512,512]{0,1:T(8,128)S(1)} fusion(bf16[8192,512]{1,0:T(8,128)(2,1)} %param.15, bf16[512,8192]{1,0:T(8,128)(2,1)} %all-gather.2.cloned.1.call-done, f32[8192]{0:T(1024)S(1)} %copy-done.6, f32[512]{0:T(512)S(1)} %add_rsqrt_fusion), kind=kOutput, calls=%fused_computation.59 | convolution fusion | flops 4307812352 | bytes 17860608 | tf_op jit(solution)/shard_map/dot_general | solution.py:84
  174.9 23.8 %multiply_bitcast_fusion = f32[64,8,16,128]{3,1,2,0:T(8,128)S(1)} fusion(bf16[8192,2048]{1,0:T(8,128)(2,1)} %param.14, bf16[512,8192]{1,0:T(8,128)(2,1)} %all-gather.2.cloned.1.call-done, f32[8192]{0:T(1024)S(1)} %copy-done.6, f32[512]{0:T(512)S(1)} %add_rsqrt_fusion), kind=kOutput, calls=%fused_computation.54 | convolution fusion | flops 17193500672 | bytes 46172160 | tf_op jit(solution)/shard_map/dot_general | solution.py:83
  211.1 17.3 %conditional.2 = (f32[2,8,512]{2,1,0:T(8,128)}, f32[2,8,512]{2,1,0:T(8,128)S(1)}, f32[2,8,512,128]{3,2,1,0:T(8,128)}) conditional(s32[]{:T(128)} %convert_element_type.75, () %tuple.45, (s32[]{:T(128)}, s32[512]{0:T(512)S(1)}, bf16[512,2,128]{2,0,1:T(8,128)(2,1)S(1)}, bf16[512,2,8,128]{3,0,2,1:T(8,128)(2,1)S(1)}, ...), branch_computations={%region_2.3_spmd, %region_3.6_spmd} | conditional | flops 2203616768 | bytes 58563616 | solution.py:60
  215.2 7.7 %broadcast_add_fusion = f32[2,8,512,128]{3,2,1,0:T(8,128)} fusion(f32[2,8,512]{2,1,0:T(8,128)S(1)} %get-tuple-element.388, f32[2,512,512,8]{2,1,3,0:T(8,128)S(1)} %get-tuple-element.393, f32[2,8,512]{2,1,0:T(8,128)} %get-tuple-element.488, pred[512,512]{0,1:T(8,128)(4,1)S(1)} %compare_and_fusion, bf16[512,2,1,128]{3,0,1,2:T(8,128)(2,1)S(1)} %get-tuple-element.287), kind=kOutput, calls=%fused_computation.8 | convolution fusion | flops 1095761920 | bytes 21561344 | tf_op jit(solution)/shard_map/cond/branch_1_fun/hgcn,nhd->hgcd/dot_general | solution.py:52
  228.4 213.8 %while.24 = (s32[]{:T(128)}, bf16[512,512]{0,1:T(8,128)(2,1)}, f32[2,8,512]{2,1,0:T(8,128)}, f32[2,8,512]{2,1,0:T(8,128)S(1)}, f32[2,8,512,128]{3,2,1,0:T(8,128)...) while((s32[]{:T(128)}, bf16[512,512]{0,1:T(8,128)(2,1)}, ...), condition=%wide.region_11.12_spmd.clone, body=%wide.region_6.11_spmd.clone.sunk | while | flops 2204911616 | bytes 71841392 | solution.py:144
  238.0 18.9 %conditional.5 = ((f32[2,8,512]{2,1,0:T(8,128)}, f32[2,8,512]{2,1,0:T(8,128)S(1)}, f32[2,8,512,128]{3,2,1,0:T(8,128)})) conditional(s32[]{:T(128)} %convert_element_type.117, (f32[2,8,512]{2,1,0:T(8,128)}, f32[2,8,512]{2,1,0:T(8,128)S(1)}, f32[2,8,512,128]{3,2,1,0:T(8,128)}) %tuple.74, (s32[]{:T(128)}, s32[]{:T(128)}, bf16[512,512]{0,1:T(8,128)(2,1)}, ...), branch_computations={%region_7.7_spmd, %region_8.10_spmd} | conditional | flops 2204649472 | bytes 62925868 | solution.py:60
  247.8 8.5 %multiply_add_fusion = f32[2,8,512,128]{3,2,1,0:T(8,128)} fusion(f32[2,8,512,128]{3,2,1,0:T(8,128)} %get-tuple-element.294, f32[2,8,512]{2,1,0:T(8,128)S(1)} %get-tuple-element.391, f32[2,512,512,8]{2,1,3,0:T(8,128)S(1)} %get-tuple-element.395, f32[2,8,512]{2,1,0:T(8,128)S(1)} %max.14, pred[512,512]{0,1:T(8,128)(4,1)S(1)} %compare_and_fusion.1, ...), kind=kOutput, calls=%fused_computation.29 | convolution fusion | flops 1096810496 | bytes 25755648 | tf_op jit(solution)/shard_map/while/body/eval_jaxpr/cond/branch_1_fun/hgcn,nhd->hgcd/dot_general | solution.py:52
  267.4 18.9 %conditional.5 = ((f32[2,8,512]{2,1,0:T(8,128)}, f32[2,8,512]{2,1,0:T(8,128)S(1)}, f32[2,8,512,128]{3,2,1,0:T(8,128)})) conditional(s32[]{:T(128)} %convert_element_type.117, (f32[2,8,512]{2,1,0:T(8,128)}, f32[2,8,512]{2,1,0:T(8,128)S(1)}, f32[2,8,512,128]{3,2,1,0:T(8,128)}) %tuple.74, (s32[]{:T(128)}, s32[]{:T(128)}, bf16[512,512]{0,1:T(8,128)(2,1)}, ...), branch_computations={%region_7.7_spmd, %region_8.10_spmd} | conditional | flops 2204649472 | bytes 62925868 | solution.py:60
  277.2 8.5 %multiply_add_fusion = f32[2,8,512,128]{3,2,1,0:T(8,128)} fusion(f32[2,8,512,128]{3,2,1,0:T(8,128)} %get-tuple-element.294, f32[2,8,512]{2,1,0:T(8,128)S(1)} %get-tuple-element.391, f32[2,512,512,8]{2,1,3,0:T(8,128)S(1)} %get-tuple-element.395, f32[2,8,512]{2,1,0:T(8,128)S(1)} %max.14, pred[512,512]{0,1:T(8,128)(4,1)S(1)} %compare_and_fusion.1, ...), kind=kOutput, calls=%fused_computation.29 | convolution fusion | flops 1096810496 | bytes 25755648 | tf_op jit(solution)/shard_map/while/body/eval_jaxpr/cond/branch_1_fun/hgcn,nhd->hgcd/dot_general | solution.py:52
  296.7 18.9 %conditional.5 = ((f32[2,8,512]{2,1,0:T(8,128)}, f32[2,8,512]{2,1,0:T(8,128)S(1)}, f32[2,8,512,128]{3,2,1,0:T(8,128)})) conditional(s32[]{:T(128)} %convert_element_type.117, (f32[2,8,512]{2,1,0:T(8,128)}, f32[2,8,512]{2,1,0:T(8,128)S(1)}, f32[2,8,512,128]{3,2,1,0:T(8,128)}) %tuple.74, (s32[]{:T(128)}, s32[]{:T(128)}, bf16[512,512]{0,1:T(8,128)(2,1)}, ...), branch_computations={%region_7.7_spmd, %region_8.10_spmd} | conditional | flops 2204649472 | bytes 62925868 | solution.py:60
  306.6 8.5 %multiply_add_fusion = f32[2,8,512,128]{3,2,1,0:T(8,128)} fusion(f32[2,8,512,128]{3,2,1,0:T(8,128)} %get-tuple-element.294, f32[2,8,512]{2,1,0:T(8,128)S(1)} %get-tuple-element.391, f32[2,512,512,8]{2,1,3,0:T(8,128)S(1)} %get-tuple-element.395, f32[2,8,512]{2,1,0:T(8,128)S(1)} %max.14, pred[512,512]{0,1:T(8,128)(4,1)S(1)} %compare_and_fusion.1, ...), kind=kOutput, calls=%fused_computation.29 | convolution fusion | flops 1096810496 | bytes 25755648 | tf_op jit(solution)/shard_map/while/body/eval_jaxpr/cond/branch_1_fun/hgcn,nhd->hgcd/dot_general | solution.py:52
  319.4 5.3 %collective-permute-done = bf16[512,512]{0,1:T(8,128)(2,1)} collective-permute-done((bf16[512,512]{0,1:T(8,128)(2,1)}, bf16[512,512]{0,1:T(8,128)(2,1)}, u32[]{:S(2)}, u32[]{:S(2)}) %collective-permute-start) | collective-permute-done | bytes 524320 | tf_op jit(solution)/shard_map/while/body/eval_jaxpr/ppermute | solution.py:12
  325.8 18.9 %conditional.5 = ((f32[2,8,512]{2,1,0:T(8,128)}, f32[2,8,512]{2,1,0:T(8,128)S(1)}, f32[2,8,512,128]{3,2,1,0:T(8,128)})) conditional(s32[]{:T(128)} %convert_element_type.117, (f32[2,8,512]{2,1,0:T(8,128)}, f32[2,8,512]{2,1,0:T(8,128)S(1)}, f32[2,8,512,128]{3,2,1,0:T(8,128)}) %tuple.74, (s32[]{:T(128)}, s32[]{:T(128)}, bf16[512,512]{0,1:T(8,128)(2,1)}, ...), branch_computations={%region_7.7_spmd, %region_8.10_spmd} | conditional | flops 2204649472 | bytes 62925868 | solution.py:60
  335.7 8.5 %multiply_add_fusion = f32[2,8,512,128]{3,2,1,0:T(8,128)} fusion(f32[2,8,512,128]{3,2,1,0:T(8,128)} %get-tuple-element.294, f32[2,8,512]{2,1,0:T(8,128)S(1)} %get-tuple-element.391, f32[2,512,512,8]{2,1,3,0:T(8,128)S(1)} %get-tuple-element.395, f32[2,8,512]{2,1,0:T(8,128)S(1)} %max.14, pred[512,512]{0,1:T(8,128)(4,1)S(1)} %compare_and_fusion.1, ...), kind=kOutput, calls=%fused_computation.29 | convolution fusion | flops 1096810496 | bytes 25755648 | tf_op jit(solution)/shard_map/while/body/eval_jaxpr/cond/branch_1_fun/hgcn,nhd->hgcd/dot_general | solution.py:52
  348.5 8.1 %collective-permute-done = bf16[512,512]{0,1:T(8,128)(2,1)} collective-permute-done((bf16[512,512]{0,1:T(8,128)(2,1)}, bf16[512,512]{0,1:T(8,128)(2,1)}, u32[]{:S(2)}, u32[]{:S(2)}) %collective-permute-start) | collective-permute-done | bytes 524320 | tf_op jit(solution)/shard_map/while/body/eval_jaxpr/ppermute | solution.py:12
  357.7 18.9 %conditional.5 = ((f32[2,8,512]{2,1,0:T(8,128)}, f32[2,8,512]{2,1,0:T(8,128)S(1)}, f32[2,8,512,128]{3,2,1,0:T(8,128)})) conditional(s32[]{:T(128)} %convert_element_type.117, (f32[2,8,512]{2,1,0:T(8,128)}, f32[2,8,512]{2,1,0:T(8,128)S(1)}, f32[2,8,512,128]{3,2,1,0:T(8,128)}) %tuple.74, (s32[]{:T(128)}, s32[]{:T(128)}, bf16[512,512]{0,1:T(8,128)(2,1)}, ...), branch_computations={%region_7.7_spmd, %region_8.10_spmd} | conditional | flops 2204649472 | bytes 62925868 | solution.py:60
  367.5 8.5 %multiply_add_fusion = f32[2,8,512,128]{3,2,1,0:T(8,128)} fusion(f32[2,8,512,128]{3,2,1,0:T(8,128)} %get-tuple-element.294, f32[2,8,512]{2,1,0:T(8,128)S(1)} %get-tuple-element.391, f32[2,512,512,8]{2,1,3,0:T(8,128)S(1)} %get-tuple-element.395, f32[2,8,512]{2,1,0:T(8,128)S(1)} %max.14, pred[512,512]{0,1:T(8,128)(4,1)S(1)} %compare_and_fusion.1, ...), kind=kOutput, calls=%fused_computation.29 | convolution fusion | flops 1096810496 | bytes 25755648 | tf_op jit(solution)/shard_map/while/body/eval_jaxpr/cond/branch_1_fun/hgcn,nhd->hgcd/dot_general | solution.py:52
  380.3 8.1 %collective-permute-done = bf16[512,512]{0,1:T(8,128)(2,1)} collective-permute-done((bf16[512,512]{0,1:T(8,128)(2,1)}, bf16[512,512]{0,1:T(8,128)(2,1)}, u32[]{:S(2)}, u32[]{:S(2)}) %collective-permute-start) | collective-permute-done | bytes 524320 | tf_op jit(solution)/shard_map/while/body/eval_jaxpr/ppermute | solution.py:12
  389.6 18.9 %conditional.5 = ((f32[2,8,512]{2,1,0:T(8,128)}, f32[2,8,512]{2,1,0:T(8,128)S(1)}, f32[2,8,512,128]{3,2,1,0:T(8,128)})) conditional(s32[]{:T(128)} %convert_element_type.117, (f32[2,8,512]{2,1,0:T(8,128)}, f32[2,8,512]{2,1,0:T(8,128)S(1)}, f32[2,8,512,128]{3,2,1,0:T(8,128)}) %tuple.74, (s32[]{:T(128)}, s32[]{:T(128)}, bf16[512,512]{0,1:T(8,128)(2,1)}, ...), branch_computations={%region_7.7_spmd, %region_8.10_spmd} | conditional | flops 2204649472 | bytes 62925868 | solution.py:60
  399.4 8.5 %multiply_add_fusion = f32[2,8,512,128]{3,2,1,0:T(8,128)} fusion(f32[2,8,512,128]{3,2,1,0:T(8,128)} %get-tuple-element.294, f32[2,8,512]{2,1,0:T(8,128)S(1)} %get-tuple-element.391, f32[2,512,512,8]{2,1,3,0:T(8,128)S(1)} %get-tuple-element.395, f32[2,8,512]{2,1,0:T(8,128)S(1)} %max.14, pred[512,512]{0,1:T(8,128)(4,1)S(1)} %compare_and_fusion.1, ...), kind=kOutput, calls=%fused_computation.29 | convolution fusion | flops 1096810496 | bytes 25755648 | tf_op jit(solution)/shard_map/while/body/eval_jaxpr/cond/branch_1_fun/hgcn,nhd->hgcd/dot_general | solution.py:52
  412.2 8.1 %collective-permute-done = bf16[512,512]{0,1:T(8,128)(2,1)} collective-permute-done((bf16[512,512]{0,1:T(8,128)(2,1)}, bf16[512,512]{0,1:T(8,128)(2,1)}, u32[]{:S(2)}, u32[]{:S(2)}) %collective-permute-start) | collective-permute-done | bytes 524320 | tf_op jit(solution)/shard_map/while/body/eval_jaxpr/ppermute | solution.py:12
  421.4 18.9 %conditional.5 = ((f32[2,8,512]{2,1,0:T(8,128)}, f32[2,8,512]{2,1,0:T(8,128)S(1)}, f32[2,8,512,128]{3,2,1,0:T(8,128)})) conditional(s32[]{:T(128)} %convert_element_type.117, (f32[2,8,512]{2,1,0:T(8,128)}, f32[2,8,512]{2,1,0:T(8,128)S(1)}, f32[2,8,512,128]{3,2,1,0:T(8,128)}) %tuple.74, (s32[]{:T(128)}, s32[]{:T(128)}, bf16[512,512]{0,1:T(8,128)(2,1)}, ...), branch_computations={%region_7.7_spmd, %region_8.10_spmd} | conditional | flops 2204649472 | bytes 62925868 | solution.py:60
  431.2 8.5 %multiply_add_fusion = f32[2,8,512,128]{3,2,1,0:T(8,128)} fusion(f32[2,8,512,128]{3,2,1,0:T(8,128)} %get-tuple-element.294, f32[2,8,512]{2,1,0:T(8,128)S(1)} %get-tuple-element.391, f32[2,512,512,8]{2,1,3,0:T(8,128)S(1)} %get-tuple-element.395, f32[2,8,512]{2,1,0:T(8,128)S(1)} %max.14, pred[512,512]{0,1:T(8,128)(4,1)S(1)} %compare_and_fusion.1, ...), kind=kOutput, calls=%fused_computation.29 | convolution fusion | flops 1096810496 | bytes 25755648 | tf_op jit(solution)/shard_map/while/body/eval_jaxpr/cond/branch_1_fun/hgcn,nhd->hgcd/dot_general | solution.py:52
  (167 shorter events, 162.4 us)
Async XLA Ops:
  7.2 155.5 %copy-start.6 = (f32[8192]{0:T(1024)S(1)}, f32[8192]{0:T(1024)}, u32[]{:S(2)}) copy-start(f32[8192]{0:T(1024)} %param.13) | copy-start | bytes 98308
  7.2 150.4 %all-gather.2.cloned.1.call-start = ((), (), s32[]{:S(2)}) async-start(), calls=%async_computation | async-start | bytes 10485760 | tf_op jit(solution)/shard_map/all_gather | solution.py:79
  172.8 1.1 copy-start.3
  203.3 6.5 %copy-start.2 = (bf16[512,2,128]{2,0,1:T(8,128)(2,1)S(1)}, bf16[512,2,128]{2,0,1:T(8,128)(2,1)}, u32[]{:S(2)}) copy-start(bf16[512,2,128]{2,0,1:T(8,128)(2,1)} %pad_maximum_fusion.2) | copy-start | bytes 786436
  203.3 6.5 %copy-start.4 = (bf16[512,2,1,128]{3,0,1,2:T(8,128)(2,1)S(1)}, bf16[512,2,1,128]{3,0,1,2:T(8,128)(2,1)}, u32[]{:S(2)}) copy-start(bf16[512,2,1,128]{3,0,1,2:T(8,128)(2,1)} %copy-done.3) | copy-start | bytes 786436
  209.8 1.3 copy-start
  228.7 7.1 %collective-permute-start = (bf16[512,512]{0,1:T(8,128)(2,1)}, bf16[512,512]{0,1:T(8,128)(2,1)}, u32[]{:S(2)}, u32[]{:S(2)}) collective-permute-start(bf16[512,512]{0,1:T(8,128)(2,1)} %get-tuple-element.511), channel_id=1, source_target_pairs={{0,4},{4,8},{8,12},{12,16},{16,20},{20,24},{24,28},{28,0},{1,5},{5... | collective-permute-start | bytes 1572872 | tf_op jit(solution)/shard_map/while/body/eval_jaxpr/ppermute | solution.py:12
  258.8 6.4 %collective-permute-start = (bf16[512,512]{0,1:T(8,128)(2,1)}, bf16[512,512]{0,1:T(8,128)(2,1)}, u32[]{:S(2)}, u32[]{:S(2)}) collective-permute-start(bf16[512,512]{0,1:T(8,128)(2,1)} %get-tuple-element.511), channel_id=1, source_target_pairs={{0,4},{4,8},{8,12},{12,16},{16,20},{20,24},{24,28},{28,0},{1,5},{5... | collective-permute-start | bytes 1572872 | tf_op jit(solution)/shard_map/while/body/eval_jaxpr/ppermute | solution.py:12
  288.1 6.4 %collective-permute-start = (bf16[512,512]{0,1:T(8,128)(2,1)}, bf16[512,512]{0,1:T(8,128)(2,1)}, u32[]{:S(2)}, u32[]{:S(2)}) collective-permute-start(bf16[512,512]{0,1:T(8,128)(2,1)} %get-tuple-element.511), channel_id=1, source_target_pairs={{0,4},{4,8},{8,12},{12,16},{16,20},{20,24},{24,28},{28,0},{1,5},{5... | collective-permute-start | bytes 1572872 | tf_op jit(solution)/shard_map/while/body/eval_jaxpr/ppermute | solution.py:12
  317.5 7.2 %collective-permute-start = (bf16[512,512]{0,1:T(8,128)(2,1)}, bf16[512,512]{0,1:T(8,128)(2,1)}, u32[]{:S(2)}, u32[]{:S(2)}) collective-permute-start(bf16[512,512]{0,1:T(8,128)(2,1)} %get-tuple-element.511), channel_id=1, source_target_pairs={{0,4},{4,8},{8,12},{12,16},{16,20},{20,24},{24,28},{28,0},{1,5},{5... | collective-permute-start | bytes 1572872 | tf_op jit(solution)/shard_map/while/body/eval_jaxpr/ppermute | solution.py:12
  346.6 10.0 %collective-permute-start = (bf16[512,512]{0,1:T(8,128)(2,1)}, bf16[512,512]{0,1:T(8,128)(2,1)}, u32[]{:S(2)}, u32[]{:S(2)}) collective-permute-start(bf16[512,512]{0,1:T(8,128)(2,1)} %get-tuple-element.511), channel_id=1, source_target_pairs={{0,4},{4,8},{8,12},{12,16},{16,20},{20,24},{24,28},{28,0},{1,5},{5... | collective-permute-start | bytes 1572872 | tf_op jit(solution)/shard_map/while/body/eval_jaxpr/ppermute | solution.py:12
  378.5 10.0 %collective-permute-start = (bf16[512,512]{0,1:T(8,128)(2,1)}, bf16[512,512]{0,1:T(8,128)(2,1)}, u32[]{:S(2)}, u32[]{:S(2)}) collective-permute-start(bf16[512,512]{0,1:T(8,128)(2,1)} %get-tuple-element.511), channel_id=1, source_target_pairs={{0,4},{4,8},{8,12},{12,16},{16,20},{20,24},{24,28},{28,0},{1,5},{5... | collective-permute-start | bytes 1572872 | tf_op jit(solution)/shard_map/while/body/eval_jaxpr/ppermute | solution.py:12
  410.3 10.0 %collective-permute-start = (bf16[512,512]{0,1:T(8,128)(2,1)}, bf16[512,512]{0,1:T(8,128)(2,1)}, u32[]{:S(2)}, u32[]{:S(2)}) collective-permute-start(bf16[512,512]{0,1:T(8,128)(2,1)} %get-tuple-element.511), channel_id=1, source_target_pairs={{0,4},{4,8},{8,12},{12,16},{16,20},{20,24},{24,28},{28,0},{1,5},{5... | collective-permute-start | bytes 1572872 | tf_op jit(solution)/shard_map/while/body/eval_jaxpr/ppermute | solution.py:12
  442.2 6.2 %copy-start.1 = (bf16[2048,512]{1,0:T(8,128)(2,1)S(1)}, bf16[2048,512]{1,0:T(8,128)(2,1)}, u32[]{:S(2)}) copy-start(bf16[2048,512]{1,0:T(8,128)(2,1)} %get-tuple-element.323) | copy-start | bytes 6291460
  442.2 6.2 %copy-start.5 = (pred[2048]{0:T(1024)(128)(4,1)S(1)}, pred[2048]{0:T(1024)(128)(4,1)}, u32[]{:S(2)}) copy-start(pred[2048]{0:T(1024)(128)(4,1)} %add_compare_fusion) | copy-start | bytes 6148
Sparse Core Ops, SparseCore 0:
  9.6 147.9 all-gather.1
where the time goes:
time: 463 us; the launch traced here: 457 us
  waiting for transfers between devices  188 us (41%)
  matrix products  132 us (29%)
  other arithmetic  70.7 us (15%)
  local copies, waits for them, and re-layouts  45.3 us (10%)
  between operations  15.5 us (3%)
    all_gather x1, waiting for transfers between devices, local(): whole = lax.all_gather(tokens, 'tp', axis=1, tiled=True)  144 us
    dot_general x8, matrix products, run(): jnp.einsum('hgcn,nhd->hgcd', weights, vblock, preferred_element_type=jnp....  67 us
    ppermute x7, waiting for transfers between devices, passed_along(): lax.ppermute(x, axis, [(i, (i + by) % length) for i in range(length)])  43.4 us
    reduce_sum x8, other arithmetic, run(): total = total * factor + jnp.sum(prob, axis=-1)  32.6 us
    dot_general x8, matrix products, run(): jnp.einsum('chgd,nhd->hgcn', query_set, kblock, preferred_element_type=jn...  31.2 us
    dot_general x1, matrix products, local(): query = jnp.dot(normed, w_query, preferred_element_type=jnp.float32)  23.8 us
    select_n x28, local copies, waits for them, and re-layouts, place(): return jnp.where(owned, updated, handed_now)  16.3 us
    while x7, local copies, waits for them, and re-layouts  13.2 us
  transfers between devices with their start and end apart: 8, of which 8 were waited for; matrix products, arithmetic and copies ran while one was open for 3% of the time, Pallas kernels for 0%

commit v1 on v0

v1 whole, which is shorter than its diff:
```python
import functools
import math

import jax
import jax.numpy as jnp
from jax import lax
from jax.experimental import pallas as pl
from jax.experimental.pallas import tpu as pltpu
from jax.sharding import PartitionSpec as P

HEAD_SIZE = 128
GROUPS = 4
TILE = 64
DEPTH = 512
KEYS = 512
VMEM = 56 * 1024 * 1024
LOW = -1e30


def shifted(x, axis, by):
    n = lax.axis_size(axis)
    return lax.ppermute(x, axis, [(i, (i + by) % n) for i in range(n)])


def paired(x, axis, mask):
    return lax.ppermute(x, axis, [(i, i ^ mask) for i in range(lax.axis_size(axis))])


def cut(x, start, rows, after):
    def body(x_ref, *refs):
        refs[-1][...] = x_ref[...]

    return pl.pallas_call(
        body,
        grid=(rows // TILE,),
        in_specs=[pl.BlockSpec((TILE, x.shape[1]), lambda i: (start // TILE + i, 0))]
        + [pl.BlockSpec(memory_space=pl.ANY)] * len(after),
        out_specs=pl.BlockSpec((TILE, x.shape[1]), lambda i: (i, 0)),
        out_shape=jax.ShapeDtypeStruct((rows, x.shape[1]), x.dtype),
    )(x, *after)


def project(parts, order, gain, weights, carry, tables, name):
    count = len(parts)
    rows = sum(p.shape[0] for p in parts[0])
    width = parts[0][0].shape[1]
    steps = width // DEPTH
    model = weights[0][0].shape[0]
    n_weights = len(weights)
    flat = [p for part in parts for p in part]

    def body(order_ref, *refs):
        refs = list(refs)
        part_refs = [[refs.pop(0) for _ in part] for part in parts]
        gain_ref = refs.pop(0)
        w_refs = [refs.pop(0) for _ in weights]
        carry_refs = [refs.pop(0) for _ in range(n_weights + 1)] if carry else None
        table_refs = [refs.pop(0) for _ in range(2)] if tables else None
        outs = [refs.pop(0) for _ in range(n_weights if tables else n_weights + 1)]
        x_ref = refs.pop(0)
        sums = refs if tables else outs
        step = pl.program_id(0)

        @pl.when(step == 0)
        def _():
            for i, s in enumerate(sums):
                s[...] = carry_refs[i][...] if carry else jnp.zeros_like(s)

        for i in range(count):

            @pl.when(step // steps == i)
            def _():
                at = 0
                for ref in part_refs[i]:
                    x_ref[at : at + ref.shape[0], :] = ref[...]
                    at += ref.shape[0]

        x = x_ref[...].astype(jnp.float32)
        normed = (x * gain_ref[0]).astype(jnp.bfloat16)
        square = x * x
        sums[-1][...] += sum(square[:, i : i + 128] for i in range(0, DEPTH, 128))
        for s, w in zip(sums, w_refs):
            s[...] += jnp.dot(normed, w[...], preferred_element_type=jnp.float32)

        if tables:

            @pl.when(step == count * steps - 1)
            def _():
                mean = jnp.sum(sums[-1][...], axis=1, keepdims=True) / model
                inv = lax.rsqrt(mean + 1e-05)
                cosine, sine = table_refs[0][...], table_refs[1][...]
                for s, out, (_, turned) in zip(sums, outs, weights):
                    for h, turn in enumerate(turned):
                        u = s[:, h * 128 : h * 128 + 128] * inv
                        if turn:
                            u = u * cosine + pltpu.roll(u, 64, 1) * sine
                        out[:, h * 128 : h * 128 + 128] = u.astype(jnp.bfloat16)

    def part_spec(i, p):
        return pl.BlockSpec(
            (p.shape[0], DEPTH), lambda s, order: (0, jnp.clip(s - i * steps, 0, steps - 1))
        )

    def block(s, order):
        return order[s // steps] * steps + s % steps

    def whole(a):
        return pl.BlockSpec(a.shape, lambda s, order: (0,) * len(a.shape))

    columns = [w.shape[1] for w, _ in weights]
    sum_shapes = [(rows, c) for c in columns] + [(rows, 128)]
    in_specs = [part_spec(i, p) for i, part in enumerate(parts) for p in part]
    in_specs += [pl.BlockSpec((1, 1, DEPTH), lambda s, order: (block(s, order), 0, 0))]
    in_specs += [
        pl.BlockSpec((DEPTH, c), lambda s, order: (block(s, order), 0)) for c in columns
    ]
    extra = list(carry or ()) + list(tables or ())
    in_specs += [whole(a) for a in extra]
    if tables:
        out_shape = [jax.ShapeDtypeStruct((rows, c), jnp.bfloat16) for c in columns]
        scratch = [pltpu.VMEM(s, jnp.float32) for s in sum_shapes]
    else:
        out_shape = [jax.ShapeDtypeStruct(s, jnp.float32) for s in sum_shapes]
        scratch = []
    moved = count * width * sum(columns) * 2
    return pl.pallas_call(
        body,
        grid_spec=pltpu.PrefetchScalarGridSpec(
            num_scalar_prefetch=1,
            grid=(count * steps,),
            in_specs=in_specs,
            out_specs=[whole(s) for s in out_shape],
            scratch_shapes=[pltpu.VMEM((rows, DEPTH), jnp.bfloat16)] + scratch,
        ),
        out_shape=out_shape,
        name=name,
        cost_estimate=pl.CostEstimate(
            flops=2 * rows * count * width * sum(columns), bytes_accessed=moved, transcendentals=0
        ),
        compiler_params=pltpu.CompilerParams(vmem_limit_bytes=VMEM),
    )(order, *flat, gain.reshape(model // DEPTH, 1, DEPTH), *[w for w, _ in weights], *extra)


def stacked(q_ref, ratio):
    return jnp.concatenate(
        [q_ref[:, h * HEAD_SIZE : (h + 1) * HEAD_SIZE] for h in range(ratio)], axis=0
    )


def scale():
    return math.log2(math.e) / math.sqrt(HEAD_SIZE)


def first_block(q, k, v, valid, state):
    s = lax.dot_general(q, k, (((1,), (1,)), ((), ())), preferred_element_type=jnp.float32)
    s = jnp.where(valid, s, LOW)
    top = jnp.max(s, axis=1, keepdims=True)
    p = jnp.exp2((s - top) * scale()).astype(jnp.bfloat16)
    fresh = jnp.dot(p, v, preferred_element_type=jnp.float32)
    keep_top(state, fresh, top)


def keep_top(state, sums, top):
    lane = lax.broadcasted_iota(jnp.int32, sums.shape, 1)
    state[...] = jnp.where(lane < HEAD_SIZE + 64, sums, top)


def next_block(q, kt, v, valid, state):
    s = jnp.dot(q, kt, preferred_element_type=jnp.float32)
    if valid is not None:
        s = jnp.where(valid, s, LOW)
    old = state[:, 2 * HEAD_SIZE - 1 :]
    top = jnp.maximum(old, jnp.max(s, axis=1, keepdims=True))
    p = jnp.exp2((s - top) * scale()).astype(jnp.bfloat16)
    fresh = state[...] * jnp.exp2((old - top) * scale())
    fresh += jnp.dot(p, v, preferred_element_type=jnp.float32)
    keep_top(state, fresh, top)


def over_keys(q, load, valid_count, state):
    full = valid_count // KEYS

    def one(i, _):
        kt, v = load(i)
        next_block(q, kt, v, None, state)
        return 0

    lax.fori_loop(0, full, one, 0)

    @pl.when(valid_count % KEYS > 0)
    def _():
        kt, v = load(full)
        column = lax.broadcasted_iota(jnp.int32, (q.shape[0], KEYS), 1)
        next_block(q, kt, v, column < valid_count - full * KEYS, state)


def with_ones(v):
    return jnp.concatenate([v, jnp.ones_like(v)], axis=1)


def attend_early(place, query, own, sets, state, start, rows, total_rows):
    kv_local = own.shape[1] // (2 * HEAD_SIZE)
    ratio = query.shape[1] // HEAD_SIZE // kv_local
    height = ratio * TILE
    n_sets = len(sets)

    def body(place_ref, q_ref, own_ref, *refs):
        set_refs = refs[:n_sets]
        out = refs[-1].at[0, 0]
        t, g = pl.program_id(0), pl.program_id(1)
        me = place_ref[0]
        q = stacked(q_ref, ratio)
        k, v = own_ref[:, :HEAD_SIZE], own_ref[:, HEAD_SIZE:]
        row = lax.broadcasted_iota(jnp.int32, (height, rows), 0) % TILE + t * TILE
        column = lax.broadcasted_iota(jnp.int32, (height, rows), 1)
        first_block(q, k, with_ones(v), column <= row, out)
        for ref, (_, set_rows) in zip(set_refs, sets):

            def load(i, ref=ref):
                at = pl.ds(pl.multiple_of(i * KEYS, KEYS), KEYS)
                return ref[at, :HEAD_SIZE].T, with_ones(ref[at, HEAD_SIZE:])

            over_keys(q, load, (me + 1) * set_rows, out)

    tiles = total_rows // TILE
    state_shape = jax.ShapeDtypeStruct((tiles, kv_local, height, 2 * HEAD_SIZE), jnp.float32)
    in_specs = [
        pl.BlockSpec((TILE, ratio * HEAD_SIZE), lambda t, g, place: (t, g)),
        pl.BlockSpec((rows, 2 * HEAD_SIZE), lambda t, g, place: (0, g)),
    ]
    in_specs += [
        pl.BlockSpec((s.shape[0], 2 * HEAD_SIZE), lambda t, g, place: (0, g)) for s, _ in sets
    ]
    args = [query, own] + [s for s, _ in sets]
    aliases = {}
    if state is not None:
        aliases = {1 + len(args): 0}
        in_specs.append(pl.BlockSpec(memory_space=pl.ANY))
        args.append(state)
    keys = sum(s.shape[0] for s, _ in sets) + rows
    return pl.pallas_call(
        body,
        grid_spec=pltpu.PrefetchScalarGridSpec(
            num_scalar_prefetch=1,
            grid=(rows // TILE, kv_local),
            in_specs=in_specs,
            out_specs=pl.BlockSpec(
                (1, 1, height, 2 * HEAD_SIZE), lambda t, g, place: (start // TILE + t, g, 0, 0)
            ),
        ),
        out_shape=state_shape,
        input_output_aliases=aliases,
        name=f"early_{start}",
        cost_estimate=pl.CostEstimate(
            flops=8 * keys * rows * query.shape[1],
            bytes_accessed=keys * 1024,
            transcendentals=0,
        ),
        compiler_params=pltpu.CompilerParams(vmem_limit_bytes=VMEM),
    )(place, *args)


def attend_late(place, queries, own, near, far, far_near, state, cache, start, total_rows, last):
    rows = own.shape[0]
    kv_width = own.shape[1]
    kv_local = kv_width // (2 * HEAD_SIZE)
    ratio = queries[0].shape[1] // HEAD_SIZE // kv_local
    height = ratio * TILE
    others = far.shape[0] // rows
    chain = 2 * others + 2
    n_keys = chain * rows
    tiles = (start + rows) // TILE
    firsts = []
    at = 0
    for q in queries:
        firsts.append(at)
        at += q.shape[0] // TILE

    def body(place_ref, *refs):
        refs = list(refs)
        q_refs = [refs.pop(0) for _ in queries]
        own_ref, near_ref, far_ref, far_near_ref, state_ref = [refs.pop(0) for _ in range(5)]
        if cache is not None:
            refs.pop(0)
        if last:
            out, cache_out, kv, kt_ref, v_ref, q_scr, st = refs
        else:
            out, cache_out, kv, kt_ref, v_ref, q_scr = refs
            st = out.at[0, 0]
        t, g = pl.program_id(0), pl.program_id(1)
        me, length, span = place_ref[0], place_ref[1], place_ref[2]

        @pl.when((t == 0) & (g == 0))
        def _():
            def put(stretch, value):
                kv[pl.ds(pl.multiple_of(stretch * rows, rows), rows), :] = value

            put(me, own_ref[...])
            put(me ^ 1, near_ref[...])
            for i in range(others):
                put(me ^ (2 * i + 2), far_ref[i * rows : (i + 1) * rows, :])
                put(me ^ (2 * i + 3), far_near_ref[i * rows : (i + 1) * rows, :])
            for h in range(kv_local):
                base = h * 2 * HEAD_SIZE
                for b in range(0, n_keys, KEYS):
                    kt_ref[h, b // KEYS] = kv[b : b + KEYS, base : base + HEAD_SIZE].T
                v_ref[h] = with_ones(kv[:, base + HEAD_SIZE : base + 2 * HEAD_SIZE])

        piece = jnp.minimum(t, rows // TILE - 1) * TILE
        for j in range(GROUPS):
            at = pl.multiple_of((span + j) * rows + piece, TILE)
            index = (span + j) * total_rows + start + piece
            index += lax.broadcasted_iota(jnp.int32, (TILE, kv_width), 0)
            value = kv[pl.ds(at, TILE), :]
            cache_out[j] = jnp.where(index < length, value, jnp.zeros_like(value))

        for i, ref in enumerate(q_refs):

            @pl.when((t >= firsts[i]) & (t < firsts[i] + queries[i].shape[0] // TILE))
            def _():
                q_scr[...] = stacked(ref, ratio)

        st[...] = state_ref[0, 0]

        def load(i):
            return kt_ref[g, i], v_ref[g, pl.ds(pl.multiple_of(i * KEYS, KEYS), KEYS), :]

        over_keys(q_scr[...], load, me * rows, st)
        if last:
            done = st[:, :HEAD_SIZE] / st[:, HEAD_SIZE : HEAD_SIZE + 1]
            for h in range(ratio):
                out[:, h * HEAD_SIZE : (h + 1) * HEAD_SIZE] = done[
                    h * TILE : (h + 1) * TILE
                ].astype(jnp.bfloat16)

    def whole(a):
        return pl.BlockSpec(a.shape, lambda t, g, place: (0,) * len(a.shape))

    def q_spec(i, q):
        n = q.shape[0] // TILE
        return pl.BlockSpec(
            (TILE, ratio * HEAD_SIZE),
            lambda t, g, place: (jnp.clip(t - firsts[i], 0, n - 1), g),
        )

    state_spec = pl.BlockSpec((1, 1, height, 2 * HEAD_SIZE), lambda t, g, place: (t, g, 0, 0))
    in_specs = [q_spec(i, q) for i, q in enumerate(queries)]
    in_specs += [whole(a) for a in (own, near, far, far_near)]
    in_specs += [state_spec]
    args = list(queries) + [own, near, far, far_near, state]
    aliases = {} if last else {len(args): 0}
    if cache is not None:
        in_specs.append(pl.BlockSpec(memory_space=pl.ANY))
        args.append(cache)
        aliases[len(args)] = 1
    pieces = rows // TILE
    cache_spec = pl.BlockSpec(
        (GROUPS, TILE, kv_width),
        lambda t, g, place: (0, start // TILE + jnp.minimum(t, pieces - 1), 0),
    )
    set_shape = jax.ShapeDtypeStruct((n_keys, kv_width), jnp.bfloat16)
    cache_shape = jax.ShapeDtypeStruct((GROUPS, total_rows, kv_width), jnp.bfloat16)
    if last:
        out_shape = [
            jax.ShapeDtypeStruct((total_rows, queries[0].shape[1]), jnp.bfloat16),
            cache_shape,
        ]
        out_specs = [
            pl.BlockSpec((TILE, ratio * HEAD_SIZE), lambda t, g, place: (t, g)),
            cache_spec,
        ]
        scratch = [pltpu.VMEM(set_shape.shape, jnp.bfloat16)]
    else:
        out_shape = [jax.ShapeDtypeStruct(state.shape, jnp.float32), cache_shape, set_shape]
        out_specs = [state_spec, cache_spec, whole(set_shape)]
        scratch = []
    scratch += [
        pltpu.VMEM((kv_local, n_keys // KEYS, HEAD_SIZE, KEYS), jnp.bfloat16),
        pltpu.VMEM((kv_local, n_keys, 2 * HEAD_SIZE), jnp.bfloat16),
        pltpu.VMEM((height, HEAD_SIZE), jnp.bfloat16),
    ]
    if last:
        scratch.append(pltpu.VMEM((height, 2 * HEAD_SIZE), jnp.float32))
    return pl.pallas_call(
        body,
        grid_spec=pltpu.PrefetchScalarGridSpec(
            num_scalar_prefetch=1,
            grid=(tiles, kv_local),
            in_specs=in_specs,
            out_specs=out_specs,
            scratch_shapes=scratch,
        ),
        out_shape=out_shape,
        input_output_aliases=aliases,
        name=f"late_{start}",
        cost_estimate=pl.CostEstimate(
            flops=8 * n_keys * (start + rows) * queries[0].shape[1],
            bytes_accessed=tiles * 2 * height * 4096,
            transcendentals=0,
        ),
        compiler_params=pltpu.CompilerParams(vmem_limit_bytes=VMEM),
    )(place, *args)


def exchange(x):
    near = paired(x, "chain", 1)
    far = [paired(x, "chain", mask) for mask in range(2, lax.axis_size("chain"), 2)]
    far = jnp.concatenate(far, axis=0)
    return near, far, paired(far, "chain", 1)


def local(tokens, gain, w_query, key_value_weight, offsets, lengths):
    rows = tokens.shape[0]
    kv_local = key_value_weight.shape[1] // (2 * HEAD_SIZE)
    me = lax.axis_index("chain")
    chain = lax.axis_size("chain")
    tp = lax.axis_size("tp")
    lane = lax.axis_index("tp")

    half = HEAD_SIZE // 2
    freq = jnp.power(
        jnp.float32(500000.0), -2.0 * jnp.arange(half).astype(jnp.float32) / HEAD_SIZE
    )
    position = offsets[0] + jnp.arange(rows, dtype=jnp.int32)
    angle = position.astype(jnp.float32)[:, None] * freq[None, :]
    cosine, sine = jnp.cos(angle), jnp.sin(angle)
    cosine = jnp.concatenate([cosine, cosine], axis=1)
    sine = jnp.concatenate([-sine, sine], axis=1)

    members = chain // GROUPS
    span = me % members * GROUPS
    length = jnp.sum(jnp.where(jnp.arange(GROUPS) == me // members, lengths, 0))
    place = jnp.stack([me, length, span]).astype(jnp.int32)

    sizes = [rows * 3 // 8, rows // 4, rows // 4, rows // 8]
    starts = [sum(sizes[:i]) for i in range(len(sizes))]
    q_weight = (w_query, [True] * (w_query.shape[1] // HEAD_SIZE))
    kv_weight = (key_value_weight, [True, False] * kv_local)

    queries, sets, arrived = [], [], []
    state = cache = None
    for r, (start, size) in enumerate(zip(starts, sizes)):
        last = r == len(sizes) - 1
        tables = (cosine[start : start + size], sine[start : start + size])
        chunk = cut(tokens, start, size, arrived[r - 2] if r >= 2 else ())
        if tp == 4:
            up, down = shifted(chunk, "tp", 1), shifted(chunk, "tp", -1)
            arrived.append((up, down))
            opposite = (shifted(up[: size // 2], "tp", 1), shifted(down[size // 2 :], "tp", -1))
            order = jnp.stack([lane, (lane + 3) % 4, (lane + 1) % 4, (lane + 2) % 4])
            order = order.astype(jnp.int32)
            parts = [(chunk,), (up,), (down,), opposite]
        else:
            gathered = lax.all_gather(chunk, "tp", axis=0)
            arrived.append((gathered,))
            order = jnp.arange(tp, dtype=jnp.int32)
            parts = [(gathered[i],) for i in range(tp)]
        if last and tp == 4:
            *carry, squares = project(
                parts[:3], order[:3], gain, [q_weight, kv_weight], None, None, f"most_{start}"
            )
            (kv,) = project(
                parts[3:], order[3:], gain, [kv_weight], (carry[1], squares), tables, f"kv_{start}"
            )
            (query,) = project(
                parts[3:], order[3:], gain, [q_weight], (carry[0], squares), tables, f"q_{start}"
            )
        else:
            query, kv = project(
                parts, order, gain, [q_weight, kv_weight], None, tables, f"all_{start}"
            )
        queries.append(query)
        near, far, far_near = exchange(kv)
        state = attend_early(place, query, kv, sets, state, start, size, rows)
        got = attend_late(
            place, queries, kv, near, far, far_near, state, cache, start, rows, last
        )
        if last:
            context, cache = got
        else:
            state, cache, ready = got
            sets.append((ready, size))
    return context, cache.reshape(GROUPS * rows, key_value_weight.shape[1])


def solution(mesh):
    in_specs = (P("chain", "tp"), P(), P(None, "tp"), P(None, "tp"), P("chain"), P())
    out_specs = (P("chain", "tp"), P("chain", "tp"))
    return jax.shard_map(local, mesh=mesh, in_specs=in_specs, out_specs=out_specs, check_vma=False)
```

time: 463 us -> 399 us (0.86)
  Pallas kernels: 0 us -> 288 us
  waiting for transfers between devices: 188 us -> 43.6 us
  matrix products: 132 us -> 0 us
  other arithmetic: 70.7 us -> 7.07 us
  starting transfers between devices: 0.7 us -> 46.2 us
  local copies, waits for them, and re-layouts: 45.3 us -> 10.2 us
  between operations: 15.5 us -> 1.77 us
    pallas_call x0 -> x18, Pallas kernels: none -> 288 us  [the longest x4 104 us: attend_late(): pl.pallas_call(body, grid_spec=pltpu.PrefetchScalarGridSpec(num_scalar_pr...]
    all_gather x1 -> x0, waiting for transfers between devices: 144 us -> none  [local(): whole = lax.all_gather(tokens, 'tp', axis=1, tiled=True)]
    dot_general x18 -> x0, matrix products: 132 us -> none  [the longest x8 67 us: run(): jnp.einsum('hgcn,nhd->hgcd', weights, vblock, preferred_element_type=jnp....]
    ppermute x7 -> x36, starting transfers between devices: 0.66 us -> 46.2 us  [the longest x20 28.5 us: paired(): lax.ppermute(x, axis, [(i, i ^ mask) for i in range(lax.axis_size(axis))])]
    reduce_sum x10 -> x1, other arithmetic: 39 us -> 1.3 us  [local(): length = jnp.sum(jnp.where(jnp.arange(GROUPS) == me // members, lengths, 0))]
    select_n x28 -> x0, local copies, waits for them, and re-layouts: 16.3 us -> none  [place(): return jnp.where(owned, updated, handed_now)]
    while x7 -> x0, local copies, waits for them, and re-layouts: 13.2 us -> none
    add x17 -> x0, other arithmetic: 6.9 us -> none  [the longest x8 6.25 us: run(): total = total * factor + jnp.sum(prob, axis=-1)]
  transfers between devices with their start and end apart: 8 -> 36, of which waited for: 8 -> 8; matrix products, arithmetic and copies ran while one was open for 3% -> 3% of each run, Pallas kernels for 0% -> 66%
where the time goes in v1:
time: 399 us; the launch traced here: 397 us
  Pallas kernels  288 us (72%)
  starting transfers between devices  46.2 us (12%)
  waiting for transfers between devices  43.6 us (11%)
  local copies, waits for them, and re-layouts  10.2 us (3%)
  other arithmetic  7.07 us (2%)
    pallas_call x4, Pallas kernels, attend_late(): pl.pallas_call(body, grid_spec=pltpu.PrefetchScalarGridSpec(num_scalar_pr...  104 us
    pallas_call x6, Pallas kernels, project(): pl.pallas_call(body, grid_spec=pltpu.PrefetchScalarGridSpec(num_scalar_pr...  98.6 us
    pallas_call x4, Pallas kernels, attend_early(): pl.pallas_call(body, grid_spec=pltpu.PrefetchScalarGridSpec(num_scalar_pr...  76.8 us
    ppermute x16, waiting for transfers between devices, shifted(): return lax.ppermute(x, axis, [(i, (i + by) % n) for i in range(n)])  42.5 us
    ppermute x20, starting transfers between devices, paired(): lax.ppermute(x, axis, [(i, i ^ mask) for i in range(lax.axis_size(axis))])  28.5 us
    ppermute x16, starting transfers between devices, shifted(): return lax.ppermute(x, axis, [(i, (i + by) % n) for i in range(n)])  17.7 us
    pallas_call x4, Pallas kernels, cut(): pl.pallas_call(body, grid=(rows // TILE,), in_specs=[pl.BlockSpec((TILE,...  8.07 us
  transfers between devices with their start and end apart: 36, of which 8 were waited for; matrix products, arithmetic and copies ran while one was open for 3% of the time, Pallas kernels for 66%

profile of v1, /device:TPU:15, one launch (start us, length us, event | category | flops | bytes accessed | tf_op | source)
XLA Modules:
  0.0 396.7 jit_solution(14198412256221199026)
XLA Ops:
  3.9 2.8 shard_map.77.refs_0_
  15.4 13.3 %collective-permute-done.4.refs_1_.refs_0_ = bf16[128,2048]{1,0:T(8,128)(2,1)S(1)} collective-permute-done((bf16[128,2048]{1,0:T(8,128)(2,1)}, bf16[128,2048]{1,0:T(8,128)(2,1)S(1)}, u32[]{:S(2)}, u32[]{:S(2)}) %collective-permute-start.4) | collective-permute-done | bytes 524320 | tf_op jit(solution)/shard_map/ppermute | solution.py:22
  39.6 9.5 %collective-permute-done.14.refs_2_ = bf16[64,2048]{1,0:T(8,128)(2,1)S(1)} collective-permute-done((bf16[64,2048]{1,0:T(8,128)(2,1)}, bf16[64,2048]{1,0:T(8,128)(2,1)S(1)}, u32[]{:S(2)}, u32[]{:S(2)}) %collective-permute-start.14) | collective-permute-done | bytes 262176 | tf_op jit(solution)/shard_map/ppermute | solution.py:22
  51.6 5.8 %collective-permute-done.12.refs_1_ = bf16[64,2048]{1,0:T(8,128)(2,1)S(1)} collective-permute-done((bf16[64,2048]{1,0:T(8,128)(2,1)}, bf16[64,2048]{1,0:T(8,128)(2,1)S(1)}, u32[]{:S(2)}, u32[]{:S(2)}) %collective-permute-start.12) | collective-permute-done | bytes 262176 | tf_op jit(solution)/shard_map/ppermute | solution.py:22
  61.7 6.4 %collective-permute-done.6.refs_3_ = bf16[64,2048]{1,0:T(8,128)(2,1)S(1)} collective-permute-done((bf16[64,2048]{1,0:T(8,128)(2,1)}, bf16[64,2048]{1,0:T(8,128)(2,1)S(1)}, u32[]{:S(2)}, u32[]{:S(2)}) %collective-permute-start.6) | collective-permute-done | bytes 262176 | tf_op jit(solution)/shard_map/ppermute | solution.py:22
  68.9 23.0 %all_192.1 = (bf16[128,2048]{1,0:T(8,128)(2,1)}, bf16[128,512]{1,0:T(8,128)(2,1)}) custom-call(s32[4]{0:T(128)} %pad_add_fusion.1.order_ref, bf16[128,2048]{1,0:T(8,128)(2,1)} %shard_map.78.refs_0_, bf16[128,2048]{1,0:T(8,128)(2,1)} %copy-done.3, bf16[128,2048]{1,0:T(8,128)(2,1)} %copy-done.2, bf16[64,2048]{1,0:T(8,128)(2,1)} %copy-done.14, ...), custom_call_target="tpu_custom_call" | custom-call | flops 5368709120 | bytes 41943040 | tf_op jit(solution)/shard_map/all_192/pallas_call | solution.py:126
  92.2 17.3 %most_448.1 = (f32[64,2048]{1,0:T(8,128)}, f32[64,512]{1,0:T(8,128)}, f32[64,128]{1,0:T(8,128)}) custom-call(s32[3]{0:T(128)} %pad_add_fusion.2.order_ref, bf16[64,2048]{1,0:T(8,128)(2,1)} %shard_map.80.refs_0_, bf16[64,2048]{1,0:T(8,128)(2,1)} %copy-done.8, bf16[64,2048]{1,0:T(8,128)(2,1)} %copy-done.7, f32[16,1,512]{2,1,0:T(1,128)} %bitcast.12, ...), custom_call_target="tpu_custom_call" | custom-call | flops 2013265920 | bytes 31457280 | tf_op jit(solution)/shard_map/most_448/pallas_call | solution.py:126
  119.5 6.4 %q_448.1.q_ref.refs_3_ = bf16[64,2048]{1,0:T(8,128)(2,1)} custom-call(s32[1]{0:T(128)} %bitcast.6.order_ref, bf16[32,2048]{1,0:T(8,128)(2,1)} %copy-done.10, bf16[32,2048]{1,0:T(8,128)(2,1)} %copy-done.9, f32[16,1,512]{2,1,0:T(1,128)} %bitcast.13, bf16[8192,2048]{1,0:T(8,128)(2,1)} %refs_3_.2, f32[64,2048]{1,0:T(8,128)} %get-tuple-element.25.refs_4_, ...), custom_call_target="tpu_custom_call" | custom-call | flops 536870912 | bytes 8388608 | tf_op jit(solution)/shard_map/q_448/pallas_call | solution.py:126
  125.9 3.9 kv_448.1.own_ref.refs_4_
  132.5 25.0 %all_0.1 = (bf16[192,2048]{1,0:T(8,128)(2,1)}, bf16[192,512]{1,0:T(8,128)(2,1)}) custom-call(s32[4]{0:T(128)} %pad_add_fusion.1.order_ref, bf16[192,2048]{1,0:T(8,128)(2,1)} %shard_map.77.refs_0_, bf16[192,2048]{1,0:T(8,128)(2,1)} %copy-done.1, bf16[192,2048]{1,0:T(8,128)(2,1)} %copy-done, bf16[96,2048]{1,0:T(8,128)(2,1)} %copy-done.12, ...), custom_call_target="tpu_custom_call" | custom-call | flops 8053063680 | bytes 41943040 | tf_op jit(solution)/shard_map/all_0/pallas_call | solution.py:126
  160.5 2.6 collective-permute-start.11
  167.9 5.1 %collective-permute-start.16 = (bf16[64,512]{1,0:T(8,128)(2,1)S(1)}, bf16[64,512]{1,0:T(8,128)(2,1)S(1)}, u32[]{:S(2)}, u32[]{:S(2)}) collective-permute-start(bf16[64,512]{1,0:T(8,128)(2,1)S(1)} %copy-done.17), channel_id=1, source_target_pairs={{0,4},{4,0},{8,12},{12,8},{16,20},{20,16},{24,28},{28,24},{1,5},{5... | collective-permute-start | bytes 196616 | tf_op jit(solution)/shard_map/ppermute | solution.py:26
  173.1 3.1 collective-permute-done.10.refs_3_
  176.9 23.0 %all_320.1 = (bf16[128,2048]{1,0:T(8,128)(2,1)}, bf16[128,512]{1,0:T(8,128)(2,1)}) custom-call(s32[4]{0:T(128)} %pad_add_fusion.1.order_ref, bf16[128,2048]{1,0:T(8,128)(2,1)} %shard_map.79.refs_0_, bf16[128,2048]{1,0:T(8,128)(2,1)} %copy-done.6, bf16[128,2048]{1,0:T(8,128)(2,1)} %copy-done.5, bf16[64,2048]{1,0:T(8,128)(2,1)} %copy-done.16, ...), custom_call_target="tpu_custom_call" | custom-call | flops 5368709120 | bytes 41943040 | tf_op jit(solution)/shard_map/all_320/pallas_call | solution.py:126
  201.5 6.9 %early_0.1.refs_5_ = f32[8,2,512,256]{3,2,1,0:T(8,128)} custom-call(s32[3]{0:T(128)} %pad_add_fusion.place_ref, bf16[192,2048]{1,0:T(8,128)(2,1)} %get-tuple-element.22.q_ref.refs_0_, bf16[192,512]{1,0:T(8,128)(2,1)} %get-tuple-element.28.own_ref.refs_1_), custom_call_target="tpu_custom_call" | custom-call | flops 603979776 | bytes 196608 | tf_op jit(solution)/shard_map/early_0/pallas_call | solution.py:241
  209.7 4.0 %collective-permute-start.21 = (bf16[192,512]{1,0:T(8,128)(2,1)S(1)}, bf16[192,512]{1,0:T(8,128)(2,1)S(1)}, u32[]{:S(2)}, u32[]{:S(2)}) collective-permute-start(bf16[192,512]{1,0:T(8,128)(2,1)S(1)} %copy-done.18), channel_id=1, source_target_pairs={{0,4},{4,0},{8,12},{12,8},{16,20},{20,16},{24,28},{28,24},{1,5},{5... | collective-permute-start | bytes 589832 | tf_op jit(solution)/shard_map/ppermute | solution.py:26
  213.8 4.8 %collective-permute-start.30 = (bf16[384,512]{1,0:T(8,128)(2,1)S(1)}, bf16[384,512]{1,0:T(8,128)(2,1)S(1)}, u32[]{:S(2)}, u32[]{:S(2)}) collective-permute-start(bf16[384,512]{1,0:T(8,128)(2,1)S(1)} %constant_dynamic-update-slice_fusion.6.refs_4_), channel_id=1, source_target_pairs={{0,4},{4,0},{8,12},{12,8},{16,20},{20,16},{24,28},{28,24},{1,5},{5... | collective-permute-start | bytes 1179656 | tf_op jit(solution)/shard_map/ppermute | solution.py:26
  219.7 22.0 %late_0.1 = (f32[8,2,512,256]{3,2,1,0:T(8,128)}, bf16[4,512,512]{2,1,0:T(8,128)(2,1)}, bf16[1536,512]{1,0:T(8,128)(2,1)}) custom-call(s32[3]{0:T(128)} %pad_add_fusion.place_ref, bf16[192,2048]{1,0:T(8,128)(2,1)} %get-tuple-element.22.q_ref.refs_0_, bf16[192,512]{1,0:T(8,128)(2,1)} %get-tuple-element.28.own_ref.refs_1_, ...), custom_call_target="tpu_custom_call", output_to_operand_aliasing={{0}: (6, {})} | custom-call | flops 4831838208 | bytes 12582912 | tf_op jit(solution)/shard_map/late_0/pallas_call | solution.py:384
  241.7 19.4 %early_192.1.refs_6_ = f32[8,2,512,256]{3,2,1,0:T(8,128)} custom-call(s32[3]{0:T(128)} %pad_add_fusion.place_ref, bf16[128,2048]{1,0:T(8,128)(2,1)} %get-tuple-element.23.q_ref.refs_1_, bf16[128,512]{1,0:T(8,128)(2,1)} %get-tuple-element.30.own_ref.refs_2_, bf16[1536,512]{1,0:T(8,128)(2,1)} %get-tuple-element.29.refs_0_, ...), custom_call_target="tpu_custom_call", output_to_operand_aliasing={{}: (4, {})} | custom-call | flops 3489660928 | bytes 1703936 | tf_op jit(solution)/shard_map/early_192/pallas_call | solution.py:241
  262.3 24.5 %late_192.1 = (f32[8,2,512,256]{3,2,1,0:T(8,128)}, bf16[4,512,512]{2,1,0:T(8,128)(2,1)}, bf16[1024,512]{1,0:T(8,128)(2,1)}) custom-call(s32[3]{0:T(128)} %pad_add_fusion.place_ref, bf16[192,2048]{1,0:T(8,128)(2,1)} %get-tuple-element.22.q_ref.refs_0_, ...), custom_call_target="tpu_custom_call", output_to_operand_aliasing={{0}: (7, {}), {1}: (8, {})} | custom-call | flops 5368709120 | bytes 20971520 | tf_op jit(solution)/shard_map/late_192/pallas_call | solution.py:384
  286.8 29.5 %early_320.1.refs_7_ = f32[8,2,512,256]{3,2,1,0:T(8,128)} custom-call(s32[3]{0:T(128)} %pad_add_fusion.place_ref, bf16[128,2048]{1,0:T(8,128)(2,1)} %get-tuple-element.24.q_ref.refs_2_, bf16[128,512]{1,0:T(8,128)(2,1)} %get-tuple-element.34.own_ref.refs_3_, bf16[1536,512]{1,0:T(8,128)(2,1)} %get-tuple-element.29.refs_0_, ...), custom_call_target="tpu_custom_call", output_to_operand_aliasing={{}: (5, {})} | custom-call | flops 5637144576 | bytes 2752512 | tf_op jit(solution)/shard_map/early_320/pallas_call | solution.py:241
  317.1 33.2 %late_320.1 = (f32[8,2,512,256]{3,2,1,0:T(8,128)}, bf16[4,512,512]{2,1,0:T(8,128)(2,1)}, bf16[1024,512]{1,0:T(8,128)(2,1)}) custom-call(s32[3]{0:T(128)} %pad_add_fusion.place_ref, bf16[192,2048]{1,0:T(8,128)(2,1)} %get-tuple-element.22.q_ref.refs_0_, ...), custom_call_target="tpu_custom_call", output_to_operand_aliasing={{0}: (8, {}), {1}: (9, {})} | custom-call | flops 7516192768 | bytes 29360128 | tf_op jit(solution)/shard_map/late_320/pallas_call | solution.py:384
  350.2 21.0 %early_448.1.refs_8_ = f32[8,2,512,256]{3,2,1,0:T(8,128)} custom-call(s32[3]{0:T(128)} %pad_add_fusion.place_ref, bf16[64,2048]{1,0:T(8,128)(2,1)} %q_448.1.q_ref.refs_3_, bf16[64,512]{1,0:T(8,128)(2,1)} %kv_448.1.own_ref.refs_4_, bf16[1536,512]{1,0:T(8,128)(2,1)} %get-tuple-element.29.refs_0_, ...), custom_call_target="tpu_custom_call", output_to_operand_aliasing={{}: (6, {})} | custom-call | flops 3825205248 | bytes 3735552 | tf_op jit(solution)/shard_map/early_448/pallas_call | solution.py:241
  371.9 24.8 %late_448.1 = (bf16[512,2048]{1,0:T(8,128)(2,1)}, bf16[4,512,512]{2,1,0:T(8,128)(2,1)}) custom-call(s32[3]{0:T(128)} %pad_add_fusion.place_ref, bf16[192,2048]{1,0:T(8,128)(2,1)} %get-tuple-element.22.q_ref.refs_0_, bf16[128,2048]{1,0:T(8,128)(2,1)} %get-tuple-element.23.q_ref.refs_1_, ...), custom_call_target="tpu_custom_call", output_to_operand_aliasing={{1}: (10, {})} | custom-call | flops 4294967296 | bytes 33554432 | tf_op jit(solution)/shard_map/late_448/pallas_call | solution.py:384
  (162 shorter events, 57.6 us)
Async XLA Ops:
  2.6 26.2 %collective-permute-start.4 = (bf16[128,2048]{1,0:T(8,128)(2,1)}, bf16[128,2048]{1,0:T(8,128)(2,1)S(1)}, u32[]{:S(2)}, u32[]{:S(2)}) collective-permute-start(bf16[128,2048]{1,0:T(8,128)(2,1)} %shard_map.78.refs_0_), channel_id=1, source_target_pairs={{0,1},{1,2},{2,3},{3,0},{4,5},{5,6},{6,7},{7,4},{8,9},{9,10},{10,1... | collective-permute-start | bytes 1572872 | tf_op jit(solution)/shard_map/ppermute | solution.py:22
  6.7 102.8 %collective-permute-start.1 = (bf16[192,2048]{1,0:T(8,128)(2,1)}, bf16[192,2048]{1,0:T(8,128)(2,1)S(1)}, u32[]{:S(2)}, u32[]{:S(2)}) collective-permute-start(bf16[192,2048]{1,0:T(8,128)(2,1)} %shard_map.77.refs_0_), channel_id=1, source_target_pairs={{0,3},{1,0},{2,1},{3,2},{4,7},{5,4},{6,5},{7,6},{8,11},{9,8},{10,9... | collective-permute-start | bytes 2359304 | tf_op jit(solution)/shard_map/ppermute | solution.py:22
  32.0 25.4 %collective-permute-start.12 = (bf16[64,2048]{1,0:T(8,128)(2,1)}, bf16[64,2048]{1,0:T(8,128)(2,1)S(1)}, u32[]{:S(2)}, u32[]{:S(2)}) collective-permute-start(bf16[64,2048]{1,0:T(8,128)(2,1)} %shard_map.80.refs_0_), channel_id=1, source_target_pairs={{0,1},{1,2},{2,3},{3,0},{4,5},{5,6},{6,7},{7,4},{8,9},{9,10},{10,1... | collective-permute-start | bytes 786440 | tf_op jit(solution)/shard_map/ppermute | solution.py:22
  35.0 25.3 %collective-permute-start.7 = (bf16[64,2048]{1,0:T(8,128)(2,1)}, bf16[64,2048]{1,0:T(8,128)(2,1)S(1)}, u32[]{:S(2)}, u32[]{:S(2)}) collective-permute-start(bf16[64,2048]{1,0:T(8,128)(2,1)} %slice.71), channel_id=1, source_target_pairs={{0,3},{1,0},{2,1},{3,2},{4,7},{5,4},{6,5},{7,6},{8,11},{9,8},{10,9... | collective-permute-start | bytes 786440 | tf_op jit(solution)/shard_map/ppermute | solution.py:22
  36.8 31.4 %collective-permute-start.6 = (bf16[64,2048]{1,0:T(8,128)(2,1)}, bf16[64,2048]{1,0:T(8,128)(2,1)S(1)}, u32[]{:S(2)}, u32[]{:S(2)}) collective-permute-start(bf16[64,2048]{1,0:T(8,128)(2,1)} %slice.70), channel_id=1, source_target_pairs={{0,1},{1,2},{2,3},{3,0},{4,5},{5,6},{6,7},{7,4},{8,9},{9,10},{10,1... | collective-permute-start | bytes 786440 | tf_op jit(solution)/shard_map/ppermute | solution.py:22
  49.1 60.7 %collective-permute-start = (bf16[192,2048]{1,0:T(8,128)(2,1)}, bf16[192,2048]{1,0:T(8,128)(2,1)S(1)}, u32[]{:S(2)}, u32[]{:S(2)}) collective-permute-start(bf16[192,2048]{1,0:T(8,128)(2,1)} %shard_map.77.refs_0_), channel_id=1, source_target_pairs={{0,1},{1,2},{2,3},{3,0},{4,5},{5,6},{6,7},{7,4},{8,9},{9,10},{10,1... | collective-permute-start | bytes 2359304 | tf_op jit(solution)/shard_map/ppermute | solution.py:22
  57.4 57.2 %collective-permute-start.15 = (bf16[32,2048]{1,0:T(8,128)(2,1)S(1)}, bf16[32,2048]{1,0:T(8,128)(2,1)S(1)}, u32[]{:S(2)}, u32[]{:S(2)}) collective-permute-start(bf16[32,2048]{1,0:T(8,128)(2,1)S(1)} %slice.83), channel_id=1, source_target_pairs={{0,3},{1,0},{2,1},{3,2},{4,7},{5,4},{6,5},{7,6},{8,11},{9,8},{10,9... | collective-permute-start | bytes 393224 | tf_op jit(solution)/shard_map/ppermute | solution.py:22
  60.3 56.6 %collective-permute-start.13 = (bf16[32,2048]{1,0:T(8,128)(2,1)}, bf16[32,2048]{1,0:T(8,128)(2,1)S(1)}, u32[]{:S(2)}, u32[]{:S(2)}) collective-permute-start(bf16[32,2048]{1,0:T(8,128)(2,1)} %slice.82), channel_id=1, source_target_pairs={{0,1},{1,2},{2,3},{3,0},{4,5},{5,6},{6,7},{7,4},{8,9},{9,10},{10,1... | collective-permute-start | bytes 393224 | tf_op jit(solution)/shard_map/ppermute | solution.py:22
  91.9 20.6 %collective-permute-start.27 = (bf16[128,512]{1,0:T(8,128)(2,1)}, bf16[128,512]{1,0:T(8,128)(2,1)S(1)}, u32[]{:S(2)}, u32[]{:S(2)}) collective-permute-start(bf16[128,512]{1,0:T(8,128)(2,1)} %get-tuple-element.30.own_ref.refs_2_), channel_id=1, source_target_pairs={{0,8},{4,12},{8,0},{12,4},{16,24},{20,28},{24,16},{28,20},{1,9},{5... | collective-permute-start | bytes 393224 | tf_op jit(solution)/shard_map/ppermute | solution.py:26
  109.5 20.3 %collective-permute-start.28 = (bf16[128,512]{1,0:T(8,128)(2,1)S(1)}, bf16[128,512]{1,0:T(8,128)(2,1)S(1)}, u32[]{:S(2)}, u32[]{:S(2)}) collective-permute-start(bf16[128,512]{1,0:T(8,128)(2,1)S(1)} %copy-done.19), channel_id=1, source_target_pairs={{0,16},{4,20},{8,24},{12,28},{16,0},{20,4},{24,8},{28,12},{1,17},{... | collective-permute-start | bytes 393224 | tf_op jit(solution)/shard_map/ppermute | solution.py:26
  109.9 21.6 %collective-permute-start.3 = (bf16[96,2048]{1,0:T(8,128)(2,1)S(1)}, bf16[96,2048]{1,0:T(8,128)(2,1)S(1)}, u32[]{:S(2)}, u32[]{:S(2)}) collective-permute-start(bf16[96,2048]{1,0:T(8,128)(2,1)S(1)} %slice.65), channel_id=1, source_target_pairs={{0,3},{1,0},{2,1},{3,2},{4,7},{5,4},{6,5},{7,6},{8,11},{9,8},{10,9... | collective-permute-start | bytes 1179656 | tf_op jit(solution)/shard_map/ppermute | solution.py:22
  112.5 19.3 %collective-permute-start.2 = (bf16[96,2048]{1,0:T(8,128)(2,1)S(1)}, bf16[96,2048]{1,0:T(8,128)(2,1)S(1)}, u32[]{:S(2)}, u32[]{:S(2)}) collective-permute-start(bf16[96,2048]{1,0:T(8,128)(2,1)S(1)} %slice.64), channel_id=1, source_target_pairs={{0,1},{1,2},{2,3},{3,0},{4,5},{5,6},{6,7},{7,4},{8,9},{9,10},{10,1... | collective-permute-start | bytes 1179656 | tf_op jit(solution)/shard_map/ppermute | solution.py:22
  116.9 144.1 %collective-permute-start.26 = (bf16[128,512]{1,0:T(8,128)(2,1)S(1)}, bf16[128,512]{1,0:T(8,128)(2,1)S(1)}, u32[]{:S(2)}, u32[]{:S(2)}) collective-permute-start(bf16[128,512]{1,0:T(8,128)(2,1)S(1)} %copy-done.19), channel_id=1, source_target_pairs={{0,4},{4,0},{8,12},{12,8},{16,20},{20,16},{24,28},{28,24},{1,5},{5... | collective-permute-start | bytes 393224 | tf_op jit(solution)/shard_map/ppermute | solution.py:26
  129.9 29.8 %collective-permute-start.9 = (bf16[128,2048]{1,0:T(8,128)(2,1)S(1)}, bf16[128,2048]{1,0:T(8,128)(2,1)S(1)}, u32[]{:S(2)}, u32[]{:S(2)}) collective-permute-start(bf16[128,2048]{1,0:T(8,128)(2,1)S(1)} %copy-done.4), channel_id=1, source_target_pairs={{0,3},{1,0},{2,1},{3,2},{4,7},{5,4},{6,5},{7,6},{8,11},{9,8},{10,9... | collective-permute-start | bytes 1572872 | tf_op jit(solution)/shard_map/ppermute | solution.py:22
  130.4 30.0 %collective-permute-start.8 = (bf16[128,2048]{1,0:T(8,128)(2,1)S(1)}, bf16[128,2048]{1,0:T(8,128)(2,1)S(1)}, u32[]{:S(2)}, u32[]{:S(2)}) collective-permute-start(bf16[128,2048]{1,0:T(8,128)(2,1)S(1)} %copy-done.4), channel_id=1, source_target_pairs={{0,1},{1,2},{2,3},{3,0},{4,5},{5,6},{6,7},{7,4},{8,9},{9,10},{10,1... | collective-permute-start | bytes 1572872 | tf_op jit(solution)/shard_map/ppermute | solution.py:22
  131.5 26.9 %collective-permute-start.18 = (bf16[64,512]{1,0:T(8,128)(2,1)}, bf16[64,512]{1,0:T(8,128)(2,1)S(1)}, u32[]{:S(2)}, u32[]{:S(2)}) collective-permute-start(bf16[64,512]{1,0:T(8,128)(2,1)} %kv_448.1.own_ref.refs_4_), channel_id=1, source_target_pairs={{0,16},{4,20},{8,24},{12,28},{16,0},{20,4},{24,8},{28,12},{1,17},{... | collective-permute-start | bytes 196616 | tf_op jit(solution)/shard_map/ppermute | solution.py:26
  131.8 25.8 %collective-permute-start.17 = (bf16[64,512]{1,0:T(8,128)(2,1)}, bf16[64,512]{1,0:T(8,128)(2,1)S(1)}, u32[]{:S(2)}, u32[]{:S(2)}) collective-permute-start(bf16[64,512]{1,0:T(8,128)(2,1)} %kv_448.1.own_ref.refs_4_), channel_id=1, source_target_pairs={{0,8},{4,12},{8,0},{12,4},{16,24},{20,28},{24,16},{28,20},{1,9},{5... | collective-permute-start | bytes 196616 | tf_op jit(solution)/shard_map/ppermute | solution.py:26
  165.3 34.9 %collective-permute-start.19 = (bf16[64,512]{1,0:T(8,128)(2,1)S(1)}, bf16[64,512]{1,0:T(8,128)(2,1)S(1)}, u32[]{:S(2)}, u32[]{:S(2)}) collective-permute-start(bf16[64,512]{1,0:T(8,128)(2,1)S(1)} %copy-done.17), channel_id=1, source_target_pairs={{0,24},{4,28},{8,16},{12,20},{16,8},{20,12},{24,0},{28,4},{1,25},{... | collective-permute-start | bytes 196616 | tf_op jit(solution)/shard_map/ppermute | solution.py:26
  167.9 203.3 %collective-permute-start.16 = (bf16[64,512]{1,0:T(8,128)(2,1)S(1)}, bf16[64,512]{1,0:T(8,128)(2,1)S(1)}, u32[]{:S(2)}, u32[]{:S(2)}) collective-permute-start(bf16[64,512]{1,0:T(8,128)(2,1)S(1)} %copy-done.17), channel_id=1, source_target_pairs={{0,4},{4,0},{8,12},{12,8},{16,20},{20,16},{24,28},{28,24},{1,5},{5... | collective-permute-start | bytes 196616 | tf_op jit(solution)/shard_map/ppermute | solution.py:26
  173.0 45.7 %collective-permute-start.25 = (bf16[576,512]{1,0:T(8,128)(2,1)S(1)}, bf16[576,512]{1,0:T(8,128)(2,1)S(1)}, u32[]{:S(2)}, u32[]{:S(2)}) collective-permute-start(bf16[576,512]{1,0:T(8,128)(2,1)S(1)} %constant_dynamic-update-slice_fusion.3.refs_3_), channel_id=1, source_target_pairs={{0,4},{4,0},{8,12},{12,8},{16,20},{20,16},{24,28},{28,24},{1,5},{5... | collective-permute-start | bytes 1769480 | tf_op jit(solution)/shard_map/ppermute | solution.py:26
  213.8 47.7 %collective-permute-start.30 = (bf16[384,512]{1,0:T(8,128)(2,1)S(1)}, bf16[384,512]{1,0:T(8,128)(2,1)S(1)}, u32[]{:S(2)}, u32[]{:S(2)}) collective-permute-start(bf16[384,512]{1,0:T(8,128)(2,1)S(1)} %constant_dynamic-update-slice_fusion.6.refs_4_), channel_id=1, source_target_pairs={{0,4},{4,0},{8,12},{12,8},{16,20},{20,16},{24,28},{28,24},{1,5},{5... | collective-permute-start | bytes 1179656 | tf_op jit(solution)/shard_map/ppermute | solution.py:26
  218.6 152.6 %collective-permute-start.20 = (bf16[192,512]{1,0:T(8,128)(2,1)S(1)}, bf16[192,512]{1,0:T(8,128)(2,1)S(1)}, u32[]{:S(2)}, u32[]{:S(2)}) collective-permute-start(bf16[192,512]{1,0:T(8,128)(2,1)S(1)} %constant_dynamic-update-slice_fusion.refs_6_), channel_id=1, source_target_pairs={{0,4},{4,0},{8,12},{12,8},{16,20},{20,16},{24,28},{28,24},{1,5},{5... | collective-permute-start | bytes 589832 | tf_op jit(solution)/shard_map/ppermute | solution.py:26
  218.7 97.5 %collective-permute-start.31 = (bf16[128,512]{1,0:T(8,128)(2,1)S(1)}, bf16[128,512]{1,0:T(8,128)(2,1)S(1)}, u32[]{:S(2)}, u32[]{:S(2)}) collective-permute-start(bf16[128,512]{1,0:T(8,128)(2,1)S(1)} %copy-done.30), channel_id=1, source_target_pairs={{0,4},{4,0},{8,12},{12,8},{16,20},{20,16},{24,28},{28,24},{1,5},{5... | collective-permute-start | bytes 393224 | tf_op jit(solution)/shard_map/ppermute | solution.py:26
  261.1 55.2 %collective-permute-start.35 = (bf16[384,512]{1,0:T(8,128)(2,1)S(1)}, bf16[384,512]{1,0:T(8,128)(2,1)S(1)}, u32[]{:S(2)}, u32[]{:S(2)}) collective-permute-start(bf16[384,512]{1,0:T(8,128)(2,1)S(1)} %constant_dynamic-update-slice_fusion.9.refs_5_), channel_id=1, source_target_pairs={{0,4},{4,0},{8,12},{12,8},{16,20},{20,16},{24,28},{28,24},{1,5},{5... | collective-permute-start | bytes 1179656 | tf_op jit(solution)/shard_map/ppermute | solution.py:26
  (45 other events, 552.3 us)

commit v2 on v0

v2 whole, which is shorter than its diff:
```python
import math

import jax
import jax.numpy as jnp
from jax import lax
from jax.experimental import pallas as pl
from jax.experimental.pallas import tpu as pltpu
from jax.sharding import PartitionSpec as P

HEAD_SIZE = 128
GROUPS = 4
TILE = 64
FIRST = 4
KEYS = 448
SUMS = HEAD_SIZE + 16
VMEM = 63 * 1024 * 1024
SMALL = pl.CostEstimate(flops=1000, bytes_accessed=1000, transcendentals=0)
ANY = pl.BlockSpec(memory_space=pl.ANY)


def shifted(x, axis, by):
    n = lax.axis_size(axis)
    return lax.ppermute(x, axis, [(i, (i + by) % n) for i in range(n)])


def paired(x, axis, mask):
    return lax.ppermute(x, axis, [(i, i ^ mask) for i in range(lax.axis_size(axis))])


def cut(x, start, rows, after, name):
    def body(x_ref, *refs):
        out, held, sems = refs[-3:]
        for i, (a, b) in enumerate([(x_ref.at[pl.ds(start, rows), :], held), (held, out)]):
            copy = pltpu.make_async_copy(a, b, sems.at[i])
            copy.start()
            copy.wait()

    return pl.pallas_call(
        body,
        in_specs=[pl.BlockSpec(memory_space=pltpu.HBM)] + [ANY] * len(after),
        out_specs=pl.BlockSpec(memory_space=pltpu.HBM),
        out_shape=jax.ShapeDtypeStruct((rows, x.shape[1]), x.dtype),
        scratch_shapes=[
            pltpu.VMEM((rows, x.shape[1]), x.dtype),
            pltpu.SemaphoreType.DMA((2,)),
        ],
        cost_estimate=SMALL,
        name=name,
    )(x, *after)


def normed_rows(parts_refs, gain_ref, x_ref, square_ref):
    at = 0
    for ref in parts_refs:
        rows = slice(at, at + ref.shape[0])
        x = ref[...].astype(jnp.float32)
        x_ref[rows, :] = (x * gain_ref[0]).astype(jnp.bfloat16)
        square = x * x
        square_ref[rows, :] += sum(square[:, i : i + 128] for i in range(0, x.shape[1], 128))
        at += ref.shape[0]


def add_products(parts, order, gain, weights, carry, depth, after, name):
    count = len(parts)
    rows, width = parts[0].shape
    pieces = rows // TILE
    depth = min(depth, width)
    steps = width // depth
    model = weights[0].shape[0]
    n = len(weights)

    def body(order_ref, *refs):
        refs = list(refs)
        part_refs = [refs.pop(0) for _ in parts]
        gain_ref = refs.pop(0)
        w_refs = [refs.pop(0) for _ in weights]
        carry_refs = [[refs.pop(0) for _ in range(pieces)] for _ in range(n + 1)] if carry else None
        *sums, x_ref = refs[len(after) :]
        step = pl.program_id(0)

        @pl.when(step == 0)
        def _():
            for i, s in enumerate(sums):
                if carry:
                    for piece, ref in enumerate(carry_refs[i]):
                        s[piece * TILE : (piece + 1) * TILE, :] = ref[...]
                else:
                    s[...] = jnp.zeros_like(s)

        for i in range(count):

            @pl.when(step // steps == i)
            def _():
                normed_rows([part_refs[i]], gain_ref, x_ref, sums[-1])

        for s, w in zip(sums, w_refs):
            s[...] += jnp.dot(x_ref[...], w[...], preferred_element_type=jnp.float32)

    def part_spec(i):
        return pl.BlockSpec(
            (rows, depth), lambda s, order: (0, jnp.clip(s - i * steps, 0, steps - 1))
        )

    def carry_spec(columns, piece):
        return pl.BlockSpec((TILE, columns), lambda s, order: (carry[1] // TILE + piece, 0))

    def block(s, order):
        return order[s // steps] * steps + s % steps

    columns = [w.shape[1] for w in weights]
    out_shape = [jax.ShapeDtypeStruct((rows, c), jnp.float32) for c in (*columns, 128)]
    in_specs = [part_spec(i) for i in range(count)]
    in_specs += [pl.BlockSpec((1, 1, depth), lambda s, order: (block(s, order), 0, 0))]
    in_specs += [
        pl.BlockSpec((depth, c), lambda s, order: (block(s, order), 0)) for c in columns
    ]
    if carry:
        in_specs += [carry_spec(s.shape[1], p) for s in out_shape for p in range(pieces)]
    return pl.pallas_call(
        body,
        grid_spec=pltpu.PrefetchScalarGridSpec(
            num_scalar_prefetch=1,
            grid=(count * steps,),
            in_specs=in_specs + [ANY] * len(after),
            out_specs=[pl.BlockSpec(s.shape, lambda s, order: (0, 0)) for s in out_shape],
            scratch_shapes=[pltpu.VMEM((rows, depth), jnp.bfloat16)],
        ),
        out_shape=out_shape,
        name=name,
        cost_estimate=SMALL,
        compiler_params=pltpu.CompilerParams(vmem_limit_bytes=VMEM),
    )(
        order,
        *parts,
        gain.reshape(model // depth, 1, depth),
        *weights,
        *([a for a in carry[0] for _ in range(pieces)] if carry else ()),
        *after,
    )


def finish_products(part, order, gain, weight, turned, sums, squares, tables, after, name):
    width = part[0].shape[1]
    rows = sum(p.shape[0] for p in part)
    model, columns = weight.shape
    wide = min(columns, 512)

    def body(order_ref, *refs):
        refs = list(refs)
        part_refs = [refs.pop(0) for _ in part]
        gain_ref, w_ref, sums_ref, squares_ref, cosine_ref, sine_ref = refs[:6]
        out, x_ref, square_ref = refs[-3:]

        @pl.when(pl.program_id(0) == 0)
        def _():
            square_ref[...] = squares_ref[...]
            normed_rows(part_refs, gain_ref, x_ref, square_ref)
            total = jnp.sum(square_ref[...], axis=1, keepdims=True)
            square_ref[...] = jnp.broadcast_to(lax.rsqrt(total / model + 1e-05), square_ref.shape)

        inv = square_ref[...]
        sums = sums_ref[...] + jnp.dot(x_ref[...], w_ref[...], preferred_element_type=jnp.float32)
        for i, at in enumerate(range(0, wide, 128)):
            u = sums[:, at : at + 128] * inv
            if turned[i % 2]:
                u = u * cosine_ref[...] + pltpu.roll(u, 64, 1) * sine_ref[...]
            out[:, at : at + 128] = u.astype(jnp.bfloat16)

    def whole(a):
        return pl.BlockSpec(a.shape, lambda s, order: (0, 0))

    by_columns = pl.BlockSpec((rows, wide), lambda s, order: (0, s))
    return pl.pallas_call(
        body,
        grid_spec=pltpu.PrefetchScalarGridSpec(
            num_scalar_prefetch=1,
            grid=(columns // wide,),
            in_specs=[whole(p) for p in part]
            + [pl.BlockSpec((1, 1, width), lambda s, order: (order[0], 0, 0))]
            + [pl.BlockSpec((width, wide), lambda s, order: (order[0], s))]
            + [by_columns, whole(squares), whole(tables[0]), whole(tables[1])]
            + [ANY] * len(after),
            out_specs=by_columns,
            scratch_shapes=[
                pltpu.VMEM((rows, width), jnp.bfloat16),
                pltpu.VMEM((rows, 128), jnp.float32),
            ],
        ),
        out_shape=jax.ShapeDtypeStruct((rows, columns), jnp.bfloat16),
        name=name,
        cost_estimate=SMALL,
        compiler_params=pltpu.CompilerParams(vmem_limit_bytes=VMEM),
    )(order, *part, gain.reshape(model // width, 1, width), weight, sums, squares, *tables, *after)


def stacked(q_ref, tile, ratio, group=0):
    rows = slice(tile * TILE, (tile + 1) * TILE)
    heads = range(group * ratio, (group + 1) * ratio)
    return jnp.concatenate(
        [q_ref[rows, h * HEAD_SIZE : (h + 1) * HEAD_SIZE] for h in heads], axis=0
    )


def scores(k, q):
    return lax.dot_general(k, q, (((1,), (1,)), ((), ())), preferred_element_type=jnp.float32)


def fold(s, vt, state, at, first=False):
    scale = math.log2(math.e) / math.sqrt(HEAD_SIZE)
    live = HEAD_SIZE + 8
    top = jnp.max(s, axis=0, keepdims=True)
    if not first:
        old = state[live : live + 1, at]
        top = jnp.maximum(old, top)
    p = jnp.exp2((s - top) * scale).astype(jnp.bfloat16)
    fresh = jnp.dot(vt, p, preferred_element_type=jnp.float32)[:live]
    if not first:
        fresh += state[:live, at] * jnp.exp2((old - top) * scale)
    state[:live, at] = fresh
    state[live : live + 1, at] = top


def fold_all(blocks):
    work = [(k, vt, *tile) for k, vt, tiles in blocks for tile in tiles]
    ahead = scores(work[0][0], work[0][2]())
    for i, (_, vt, _, state, at) in enumerate(work):
        s = ahead
        if i + 1 < len(work):
            ahead = scores(work[i + 1][0], work[i + 1][2]())
        fold(s, vt, state, at)


def values_and_ones(v, count=None):
    if count is not None:
        row = lax.broadcasted_iota(jnp.int32, v.shape, 0)
        v = jnp.where(row < count, v, jnp.zeros_like(v))
    n = v.shape[0]
    lane = lax.broadcasted_iota(jnp.int32, (SUMS - HEAD_SIZE, n), 1)
    row = lax.broadcasted_iota(jnp.int32, (SUMS - HEAD_SIZE, n), 0)
    live = row < 8
    if count is not None:
        live = live & (lane < count)
    ones = jnp.where(live, 1.0, 0.0).astype(jnp.bfloat16)
    return jnp.concatenate([v.T, ones], axis=0)


def attend_early(place, query, own, sets, after, name):
    rows = query.shape[0]
    kv_local = own[0].shape[1] // (2 * HEAD_SIZE)
    ratio = query.shape[1] // HEAD_SIZE // kv_local
    wide = ratio * TILE
    count = rows // TILE

    def body(place_ref, q_ref, *refs):
        own_refs = refs[: len(own)]
        set_refs = refs[len(own) : len(own) + 2 * len(sets)]
        out = refs[-1]
        me = place_ref[0]
        groups = [
            [
                (
                    lambda t=t, g=g: stacked(q_ref, t, ratio, g),
                    out.at[g],
                    slice(t * wide, (t + 1) * wide),
                )
                for t in range(count)
            ]
            for g in range(kv_local)
        ]

        def own_block(ref, g):
            at = g * 2 * HEAD_SIZE
            v = ref[:, at + HEAD_SIZE : at + 2 * HEAD_SIZE]
            return ref[:, at : at + HEAD_SIZE], values_and_ones(v)

        for g, tiles in enumerate(groups):
            k, vt = own_block(own_refs[-1], g)
            for t, (q, state, at) in enumerate(tiles):
                upto = (t + 1) * TILE
                column = lax.broadcasted_iota(jnp.int32, (upto, wide), 1) % TILE + t * TILE
                key = lax.broadcasted_iota(jnp.int32, (upto, wide), 0)
                s = jnp.where(key <= column, scores(k[:upto], q()), -1e30)
                fold(s, vt[:, :upto], state, at, first=True)
        for ref in own_refs[:-1]:
            fold_all([(*own_block(ref, g), tiles) for g, tiles in enumerate(groups)])
        for i, (_, _, set_rows) in enumerate(sets):
            k_ref, vt_ref = set_refs[2 * i], set_refs[2 * i + 1]

            def one(b, _):
                at = pl.ds(pl.multiple_of(b * KEYS, 64), KEYS)
                fold_all([(k_ref[g, at, :], vt_ref[g, b], tiles) for g, tiles in enumerate(groups)])
                return 0

            lax.fori_loop(0, (me * set_rows + KEYS - 1) // KEYS, one, 0)

    def whole(a):
        return pl.BlockSpec(a.shape, lambda i, place: (0,) * len(a.shape))

    args = [query, *own, *[a for s in sets for a in s[:2]]]
    state_shape = jax.ShapeDtypeStruct((kv_local, SUMS, count * wide), jnp.float32)
    return pl.pallas_call(
        body,
        grid_spec=pltpu.PrefetchScalarGridSpec(
            num_scalar_prefetch=1,
            grid=(1,),
            in_specs=[whole(a) for a in args] + [ANY] * len(after),
            out_specs=whole(state_shape),
        ),
        out_shape=state_shape,
        name=name,
        cost_estimate=SMALL,
        compiler_params=pltpu.CompilerParams(vmem_limit_bytes=VMEM),
    )(place, *args, *after)


def attend_late(place, queries, states, arrived, rows, cache, start, total, last, after):
    kv_width = arrived[0].shape[1]
    kv_local = kv_width // (2 * HEAD_SIZE)
    ratio = queries[0].shape[1] // HEAD_SIZE // kv_local
    wide = ratio * TILE
    n_keys = sum(a.shape[0] for a in arrived)
    blocks = -(-n_keys // KEYS)
    n = len(queries)
    n_cache = 0 if cache is None else 1

    def body(place_ref, *refs):
        refs = list(refs)
        q_refs = [refs.pop(0) for _ in queries]
        state_refs = [refs.pop(0).at[0] for _ in states]
        arrived_refs = [refs.pop(0) for _ in arrived]
        for _ in range(n_cache + len(after)):
            refs.pop(0)
        cache_ref = refs.pop(0)
        if last:
            out = refs.pop(0)
            k_ref, vt_ref, kv, piece, sems, *work = refs
        else:
            work = [refs.pop(0).at[0] for _ in states]
            k_out, vt_out = refs.pop(0), refs.pop(0)
            k_ref, vt_ref, kv, piece, sems = refs
        g = pl.program_id(0)
        me, length, span = place_ref[0], place_ref[1], place_ref[2]
        count = me * rows

        def copies():
            return [
                pltpu.make_async_copy(
                    piece.at[j], cache_ref.at[j, pl.ds(start, rows), :], sems.at[j]
                )
                for j in range(GROUPS)
            ]

        @pl.when(g == 0)
        def _():
            def put(stretch, value):
                kv[pl.ds(pl.multiple_of(stretch * rows, 64), rows), :] = value

            if len(arrived) == 1:
                kv[:n_keys, :] = arrived_refs[0][...]
            else:
                for j, ref in enumerate(arrived_refs):
                    for i in range(n_keys // rows // 2):
                        put(me ^ (2 * i + j), ref[i * rows : (i + 1) * rows, :])
            for j in range(GROUPS):
                value = kv[pl.ds(pl.multiple_of((span + j) * rows, 64), rows), :]
                index = (span + j) * total + start
                index += lax.broadcasted_iota(jnp.int32, value.shape, 0)
                piece[j] = jnp.where(index < length, value, jnp.zeros_like(value))
            for c in copies():
                c.start()
            for h in range(kv_local):
                base = h * 2 * HEAD_SIZE
                for b in range(blocks):
                    k = kv[b * KEYS : (b + 1) * KEYS, base : base + HEAD_SIZE]
                    row = lax.broadcasted_iota(jnp.int32, k.shape, 0) + b * KEYS
                    stand_in = jnp.broadcast_to(kv[0:16, base : base + HEAD_SIZE][:1], k.shape)
                    k_ref[h, b * KEYS : (b + 1) * KEYS, :] = jnp.where(row < count, k, stand_in)
                    v = kv[b * KEYS : (b + 1) * KEYS, base + HEAD_SIZE : base + 2 * HEAD_SIZE]
                    vt_ref[h, b] = values_and_ones(v, count - b * KEYS)

        for s, w in zip(state_refs, work):
            w[...] = s[...]
        tiles = [
            (lambda ref=ref, t=t: stacked(ref, t, ratio), w, slice(t * wide, (t + 1) * wide))
            for ref, w in zip(q_refs, work)
            for t in range(ref.shape[0] // TILE)
        ]

        def one(b, _):
            k = k_ref[g, pl.ds(pl.multiple_of(b * KEYS, 64), KEYS), :]
            fold_all([(k, vt_ref[g, b], tiles)])
            return 0

        lax.fori_loop(0, (count + KEYS - 1) // KEYS, one, 0)
        if last:
            for i, (_, w, at) in enumerate(tiles):
                done = (w[:HEAD_SIZE, at] / w[HEAD_SIZE : HEAD_SIZE + 1, at]).T
                for h in range(ratio):
                    out[i * TILE : (i + 1) * TILE, h * HEAD_SIZE : (h + 1) * HEAD_SIZE] = done[
                        h * TILE : (h + 1) * TILE
                    ].astype(jnp.bfloat16)
        else:
            k_out[0] = k_ref[g]
            vt_out[0] = vt_ref[g]

        @pl.when(g == kv_local - 1)
        def _():
            for c in copies():
                c.wait()

    def whole(a):
        return pl.BlockSpec(a.shape, lambda g, place: (0,) * len(a.shape))

    def by_group(a):
        return pl.BlockSpec((1,) + a.shape[1:], lambda g, place: (g,) + (0,) * (len(a.shape) - 1))

    k_shape = jax.ShapeDtypeStruct((kv_local, blocks * KEYS, HEAD_SIZE), jnp.bfloat16)
    vt_shape = jax.ShapeDtypeStruct((kv_local, blocks, SUMS, KEYS), jnp.bfloat16)
    cache_shape = jax.ShapeDtypeStruct((GROUPS, total, kv_width), jnp.bfloat16)
    args = [*queries, *states, *arrived]
    in_specs = [pl.BlockSpec((q.shape[0], ratio * HEAD_SIZE), lambda g, place: (0, g)) for q in queries]
    in_specs += [by_group(s) for s in states] + [whole(a) for a in arrived]
    aliases = {}
    if cache is not None:
        args.append(cache)
        in_specs.append(ANY)
        aliases[len(args)] = 0
    scratch = [
        pltpu.VMEM(k_shape.shape, jnp.bfloat16),
        pltpu.VMEM(vt_shape.shape, jnp.bfloat16),
        pltpu.VMEM((blocks * KEYS, kv_width), jnp.bfloat16),
        pltpu.VMEM((GROUPS, rows, kv_width), jnp.bfloat16),
        pltpu.SemaphoreType.DMA((GROUPS,)),
    ]
    if last:
        out_shape = [cache_shape, jax.ShapeDtypeStruct((total, queries[0].shape[1]), jnp.bfloat16)]
        out_specs = [ANY, pl.BlockSpec((total, ratio * HEAD_SIZE), lambda g, place: (0, g))]
        scratch += [pltpu.VMEM(s.shape[1:], jnp.float32) for s in states]
    else:
        out_shape = [cache_shape, *[jax.ShapeDtypeStruct(s.shape, s.dtype) for s in states]]
        out_shape += [k_shape, vt_shape]
        out_specs = [ANY] + [by_group(s) for s in out_shape[1:]]
        for i in range(n):
            aliases[1 + n + i] = 1 + i
    return pl.pallas_call(
        body,
        grid_spec=pltpu.PrefetchScalarGridSpec(
            num_scalar_prefetch=1,
            grid=(kv_local,),
            in_specs=in_specs + [ANY] * len(after),
            out_specs=out_specs,
            scratch_shapes=scratch,
        ),
        out_shape=out_shape,
        input_output_aliases=aliases,
        name=f"late_{start}",
        cost_estimate=SMALL,
        compiler_params=pltpu.CompilerParams(vmem_limit_bytes=VMEM),
    )(place, *args, *after)


def pack(blocks, after, name):
    rows = blocks[0].shape[0]

    def body(*refs):
        for i in range(len(blocks)):
            refs[-1][i * rows : (i + 1) * rows, :] = refs[i][...]

    spec = pl.BlockSpec(memory_space=pltpu.VMEM)
    shape = (rows * len(blocks), blocks[0].shape[1])
    return pl.pallas_call(
        body,
        in_specs=[spec] * len(blocks) + [ANY] * len(after),
        out_specs=spec,
        out_shape=jax.ShapeDtypeStruct(shape, blocks[0].dtype),
        cost_estimate=SMALL,
        name=name,
    )(*blocks, *after)


def exchange(x, after, name):
    even = [x] + [paired(x, "chain", mask) for mask in range(2, lax.axis_size("chain"), 2)]
    even = pack(even, after, name)
    return even, paired(even, "chain", 1)


def local(tokens, gain, w_query, key_value_weight, offsets, lengths):
    rows = tokens.shape[0]
    kv_local = key_value_weight.shape[1] // (2 * HEAD_SIZE)
    me = lax.axis_index("chain")
    chain = lax.axis_size("chain")
    tp = lax.axis_size("tp")
    lane = lax.axis_index("tp")

    half = HEAD_SIZE // 2
    freq = jnp.power(
        jnp.float32(500000.0), -2.0 * jnp.arange(half).astype(jnp.float32) / HEAD_SIZE
    )
    position = offsets[0] + jnp.arange(rows, dtype=jnp.int32)
    angle = position.astype(jnp.float32)[:, None] * freq[None, :]
    cosine, sine = jnp.cos(angle), jnp.sin(angle)
    cosine = jnp.concatenate([cosine, cosine], axis=1)
    sine = jnp.concatenate([-sine, sine], axis=1)

    members = chain // GROUPS
    span = me % members * GROUPS
    length = jnp.sum(jnp.where(jnp.arange(GROUPS) == me // members, lengths, 0))
    place = jnp.stack([me, length, span]).astype(jnp.int32)

    sizes = [rows * FIRST // 8, rows * (8 - FIRST) // 8]
    starts = [0, sizes[0]]
    weights = (w_query, key_value_weight)
    arrived = [None] * len(sizes)

    def send(r, after):
        chunk = cut(tokens, starts[r], sizes[r], after, f"cut_{r}")
        if tp == 4:
            arrived[r] = [chunk, shifted(chunk, "tp", 1), shifted(chunk, "tp", -1)]
        else:
            arrived[r] = [lax.all_gather(chunk, "tp", axis=0)]
        return chunk

    def forward(r, i, after):
        if tp != 4:
            return arrived[r][0]
        half = sizes[r] // 2
        part = cut(arrived[r][i], (i - 1) * half, half, after, f"pass_{r}_{i}")
        arrived[r].append(shifted(part, "tp", 3 - 2 * i))
        return part

    def near(r, after):
        if tp == 4:
            parts, which, carry = arrived[r][1:3], order[1:3], (own, starts[r])
        else:
            parts, which, carry = [arrived[r][0][i] for i in range(tp - 1)], order[:-1], None
        return add_products(parts, which, gain, weights, carry, 1024, after, f"near_{r}")

    def finish(r, weight, turned, sums, squares, after, name):
        part = arrived[r][3:] if tp == 4 else [arrived[r][0][tp - 1]]
        at = slice(starts[r], starts[r] + sizes[r])
        tables = (cosine[at], sine[at])
        return finish_products(
            part, order[-1:], gain, weight, turned, sums, squares, tables, after, f"{name}_{r}"
        )

    def keys_and_queries(r, sums):
        q_sums, kv_sums, squares = sums
        kv = finish(r, key_value_weight, (True, False), kv_sums, squares, (), "kv")
        query = finish(r, w_query, (True, True), q_sums, squares, (kv,), "query")
        return kv, query

    if tp == 4:
        order = jnp.stack([lane, (lane + 3) % 4, (lane + 1) % 4, (lane + 2) % 4])
        order = order.astype(jnp.int32)
    else:
        order = jnp.arange(tp, dtype=jnp.int32)

    step = send(0, ())
    if tp == 4:
        own = add_products([tokens], order[:1], gain, weights, None, 1024, (step,), "own")
        step = own[-1]
    step = forward(0, 1, (step,))
    step = forward(0, 2, (step,))
    step = send(1, (step,))
    sums = near(0, (step,))
    kv_0, query_0 = keys_and_queries(0, sums)
    keys = exchange(kv_0, (query_0,), "pack_0")
    state_0 = attend_early(place, query_0, [kv_0], [], keys[:1], "early_0")
    step = forward(1, 1, (state_0,))
    cache, state_0, k, vt = attend_late(
        place, [query_0], [state_0], keys, sizes[0], None, 0, rows, False, (step,)
    )
    step = forward(1, 2, (k,))
    sums = near(1, (step,))
    kv_1, query_1 = keys_and_queries(1, sums)
    keys = exchange(kv_1, (query_1,), "pack_1")
    sets = [(k, vt, sizes[0])]
    state_1 = attend_early(place, query_1, [kv_0, kv_1], sets, keys[:1], "early_1")
    queries, states = [query_0, query_1], [state_0, state_1]
    cache, context = attend_late(
        place, queries, states, keys, sizes[1], cache, starts[1], rows, True, ()
    )
    return context, cache.reshape(GROUPS * rows, key_value_weight.shape[1])


def solution(mesh):
    in_specs = (P("chain", "tp"), P(), P(None, "tp"), P(None, "tp"), P("chain"), P())
    out_specs = (P("chain", "tp"), P("chain", "tp"))
    return jax.shard_map(local, mesh=mesh, in_specs=in_specs, out_specs=out_specs, check_vma=False)
```

time: 463 us -> 235 us (0.51); the launches traced: 457 us -> 233 us
  Pallas kernels: 0 us -> 152 us
  waiting for transfers between devices: 188 us -> 42.4 us
  matrix products: 132 us -> 0 us
  other arithmetic: 70.7 us -> 4.42 us
  local copies, waits for them, and re-layouts: 45.3 us -> 3.99 us
  starting transfers between devices: 0.7 us -> 29.2 us
  between operations: 15.5 us -> 1.66 us
    pallas_call x0 -> x19, Pallas kernels: none -> 152 us  [the longest x2 46.1 us: attend_late(): pl.pallas_call(body, grid_spec=pltpu.PrefetchScalarGridSpec(num_scalar_pr...]
    all_gather x1 -> x0, waiting for transfers between devices: 144 us -> none  [local(): whole = lax.all_gather(tokens, 'tp', axis=1, tiled=True)]
    dot_general x18 -> x0, matrix products: 132 us -> none  [the longest x8 67 us: run(): jnp.einsum('hgcn,nhd->hgcd', weights, vblock, preferred_element_type=jnp....]
    reduce_sum x10 -> x1, other arithmetic: 39 us -> 0.64 us  [local(): length = jnp.sum(jnp.where(jnp.arange(GROUPS) == me // members, lengths, 0))]
    ppermute x7 -> x16, starting transfers between devices: 0.66 us -> 29.2 us  [the longest x8 21.8 us: paired(): lax.ppermute(x, axis, [(i, i ^ mask) for i in range(lax.axis_size(axis))])]
    select_n x28 -> x0, local copies, waits for them, and re-layouts: 16.3 us -> none  [place(): return jnp.where(owned, updated, handed_now)]
    while x7 -> x0, local copies, waits for them, and re-layouts: 13.2 us -> none
    add x17 -> x0, other arithmetic: 6.9 us -> none  [the longest x8 6.25 us: run(): total = total * factor + jnp.sum(prob, axis=-1)]
  transfers between devices with their start and end apart: 8 -> 16, of which waited for: 8 -> 4; matrix products, arithmetic and copies ran while one was open for 3% -> 2% of each run, Pallas kernels for 0% -> 48%
where the time goes in v2:
time: 235 us; the launch traced here: 233 us
  Pallas kernels  152 us (65%)
  waiting for transfers between devices  42.4 us (18%)
  starting transfers between devices  29.2 us (12%)
  other arithmetic  4.42 us (2%)
  local copies, waits for them, and re-layouts  3.99 us (2%)
    pallas_call x2, Pallas kernels, attend_late(): pl.pallas_call(body, grid_spec=pltpu.PrefetchScalarGridSpec(num_scalar_pr...  46.1 us
    ppermute x8, waiting for transfers between devices, shifted(): return lax.ppermute(x, axis, [(i, (i + by) % n) for i in range(n)])  41.9 us
    pallas_call x3, Pallas kernels, add_products(): pl.pallas_call(body, grid_spec=pltpu.PrefetchScalarGridSpec(num_scalar_pr...  40.9 us
    pallas_call x2, Pallas kernels, attend_early(): pl.pallas_call(body, grid_spec=pltpu.PrefetchScalarGridSpec(num_scalar_pr...  25.4 us
    pallas_call x4, Pallas kernels, finish_products(): pl.pallas_call(body, grid_spec=pltpu.PrefetchScalarGridSpec(num_scalar_pr...  23 us
    ppermute x8, starting transfers between devices, paired(): lax.ppermute(x, axis, [(i, i ^ mask) for i in range(lax.axis_size(axis))])  21.8 us
    pallas_call x6, Pallas kernels, cut(): pl.pallas_call(body, in_specs=[pl.BlockSpec(memory_space=pltpu.HBM)] + [A...  12 us
    ppermute x8, starting transfers between devices, shifted(): return lax.ppermute(x, axis, [(i, (i + by) % n) for i in range(n)])  7.41 us
  transfers between devices with their start and end apart: 16, of which 4 were waited for; matrix products, arithmetic and copies ran while one was open for 2% of the time, Pallas kernels for 48%

profile of v2, /device:TPU:15, one launch (start us, length us, event | category | flops | bytes accessed | tf_op | source)
XLA Modules:
  0.0 233.5 jit_solution(2814105629729000255)
XLA Ops:
  0.6 2.2 cut_0.1.refs_4_
  4.4 11.5 %own.1 = (f32[512,2048]{1,0:T(8,128)}, f32[512,512]{1,0:T(8,128)}, f32[512,128]{1,0:T(8,128)}) custom-call(s32[1]{0:T(128)} %bitcast.4.order_ref, bf16[512,2048]{1,0:T(8,128)(2,1)} %x_ref.3, f32[8,1,1024]{2,1,0:T(1,128)} %bitcast.13, bf16[8192,2048]{1,0:T(8,128)(2,1)} %refs_3_.13, bf16[8192,512]{1,0:T(8,128)(2,1)} %refs_3_.12, bf16[256,2048]{1,0:T(8,128)(2,1)} %cut_0.1.refs_4_), custom_call_target="tpu_custom_call" | custom-call | flops 1000 | bytes 1000 | tf_op jit(solution)/shard_map/own/pallas_call | solution.py:119
  15.9 11.4 %collective-permute-done.x_ref.refs_0_ = bf16[256,2048]{1,0:T(8,128)(2,1)} collective-permute-done((bf16[256,2048]{1,0:T(8,128)(2,1)}, bf16[256,2048]{1,0:T(8,128)(2,1)}, u32[]{:S(2)}, u32[]{:S(2)}) %collective-permute-start) | collective-permute-done | bytes 1048608 | tf_op jit(solution)/shard_map/ppermute | solution.py:23
  30.6 22.0 %collective-permute-done.2.x_ref.refs_1_ = bf16[256,2048]{1,0:T(8,128)(2,1)} collective-permute-done((bf16[256,2048]{1,0:T(8,128)(2,1)}, bf16[256,2048]{1,0:T(8,128)(2,1)}, u32[]{:S(2)}, u32[]{:S(2)}) %collective-permute-start.2) | collective-permute-done | bytes 1048608 | tf_op jit(solution)/shard_map/ppermute | solution.py:23
  57.7 2.3 cut_1.1.refs_17_
  60.0 14.7 %near_0.1 = (f32[256,2048]{1,0:T(8,128)}, f32[256,512]{1,0:T(8,128)}, f32[256,128]{1,0:T(8,128)}) custom-call(s32[2]{0:T(128)} %pad_add_fusion.1.order_ref, bf16[256,2048]{1,0:T(8,128)(2,1)} %collective-permute-done.x_ref.refs_0_, bf16[256,2048]{1,0:T(8,128)(2,1)} %collective-permute-done.2.x_ref.refs_1_, f32[8,1,1024]{2,1,0:T(1,128)} %bitcast.14, ...), custom_call_target="tpu_custom_call" | custom-call | flops 1000 | bytes 1000 | tf_op jit(solution)/shard_map/near_0/pallas_call | solution.py:119
  75.6 3.6 %kv_0.1.refs_8_.refs_0_ = bf16[256,512]{1,0:T(8,128)(2,1)} custom-call(s32[1]{0:T(128)} %bitcast.3.order_ref, bf16[128,2048]{1,0:T(8,128)(2,1)} %copy-done, bf16[128,2048]{1,0:T(8,128)(2,1)} %collective-permute-done.3.refs_1_, f32[4,1,2048]{2,1,0:T(1,128)} %bitcast.15, bf16[8192,512]{1,0:T(8,128)(2,1)} %refs_3_.12, f32[256,512]{1,0:T(8,128)} %get-tuple-element.22.refs_4_, ...), custom_call_target="tpu_custom_call" | custom-call | flops 1000 | bytes 1000 | tf_op jit(solution)/shard_map/kv_0/pallas_call | solution.py:173
  79.5 2.4 %collective-permute-start.7 = (bf16[256,512]{1,0:T(8,128)(2,1)}, bf16[256,512]{1,0:T(8,128)(2,1)S(1)}, u32[]{:S(2)}, u32[]{:S(2)}) collective-permute-start(bf16[256,512]{1,0:T(8,128)(2,1)} %kv_0.1.refs_8_.refs_0_), channel_id=1, source_target_pairs={{0,24},{4,28},{8,16},{12,20},{16,8},{20,12},{24,0},{28,4},{1,25},{... | collective-permute-start | bytes 786440 | tf_op jit(solution)/shard_map/ppermute | solution.py:27
  83.3 7.9 %query_0.1.refs_4_.q_ref.refs_0_ = bf16[256,2048]{1,0:T(8,128)(2,1)} custom-call(s32[1]{0:T(128)} %bitcast.3.order_ref, bf16[128,2048]{1,0:T(8,128)(2,1)} %copy-done, bf16[128,2048]{1,0:T(8,128)(2,1)} %collective-permute-done.3.refs_1_, f32[4,1,2048]{2,1,0:T(1,128)} %bitcast.16, bf16[8192,2048]{1,0:T(8,128)(2,1)} %refs_3_.13, ...), custom_call_target="tpu_custom_call" | custom-call | flops 1000 | bytes 1000 | tf_op jit(solution)/shard_map/query_0/pallas_call | solution.py:173
  92.7 2.2 pack_0.1.refs_1_.refs_2_
  94.9 2.7 %collective-permute-start.10 = (bf16[1024,512]{1,0:T(8,128)(2,1)}, bf16[1024,512]{1,0:T(8,128)(2,1)}, u32[]{:S(2)}, u32[]{:S(2)}) collective-permute-start(bf16[1024,512]{1,0:T(8,128)(2,1)} %pack_0.1.refs_1_.refs_2_), channel_id=1, source_target_pairs={{0,4},{4,0},{8,12},{12,8},{16,20},{20,16},{24,28},{28,24},{1,5},{5... | collective-permute-start | bytes 3145736 | tf_op jit(solution)/shard_map/ppermute | solution.py:27
  100.0 5.8 %early_0.1.refs_0_.refs_1_ = f32[2,144,2048]{2,1,0:T(8,128)} custom-call(s32[3]{0:T(128)} %pad_add_fusion.place_ref, bf16[256,2048]{1,0:T(8,128)(2,1)} %query_0.1.refs_4_.q_ref.refs_0_, bf16[256,512]{1,0:T(8,128)(2,1)} %kv_0.1.refs_8_.refs_0_, bf16[1024,512]{1,0:T(8,128)(2,1)} %pack_0.1.refs_1_.refs_2_), custom_call_target="tpu_custom_call" | custom-call | flops 1000 | bytes 1000 | tf_op jit(solution)/shard_map/early_0/pallas_call | solution.py:301
  105.7 1.9 pass_1_1.1.refs_4_
  108.8 17.8 %late_0.1 = (bf16[4,512,512]{2,1,0:T(8,128)(2,1)}, f32[2,144,2048]{2,1,0:T(8,128)}, bf16[2,2240,128]{2,1,0:T(8,128)(2,1)}, bf16[2,5,144,448]{3,2,1,0:T(8,128)(2,1)}) custom-call(s32[3]{0:T(128)} %pad_add_fusion.place_ref, bf16[256,2048]{1,0:T(8,128)(2,1)} %query_0.1.refs_4_.q_ref.refs_0_, ...), custom_call_target="tpu_custom_call", output_to_operand_aliasing={{1}: (2, {})} | custom-call | flops 1000 | bytes 1000 | tf_op jit(solution)/shard_map/late_0/pallas_call | solution.py:445
  126.6 8.5 %collective-permute-done.9.x_ref.refs_1_ = bf16[256,2048]{1,0:T(8,128)(2,1)} collective-permute-done((bf16[256,2048]{1,0:T(8,128)(2,1)}, bf16[256,2048]{1,0:T(8,128)(2,1)}, u32[]{:S(2)}, u32[]{:S(2)}) %collective-permute-start.9) | collective-permute-done | bytes 1048608 | tf_op jit(solution)/shard_map/ppermute | solution.py:23
  135.1 1.9 pass_1_2.1.refs_17_
  138.2 14.7 %near_1.1 = (f32[256,2048]{1,0:T(8,128)}, f32[256,512]{1,0:T(8,128)}, f32[256,128]{1,0:T(8,128)}) custom-call(s32[2]{0:T(128)} %pad_add_fusion.1.order_ref, bf16[256,2048]{1,0:T(8,128)(2,1)} %collective-permute-done.4.x_ref.refs_0_, bf16[256,2048]{1,0:T(8,128)(2,1)} %collective-permute-done.9.x_ref.refs_1_, f32[8,1,1024]{2,1,0:T(1,128)} %bitcast.17, ...), custom_call_target="tpu_custom_call" | custom-call | flops 1000 | bytes 1000 | tf_op jit(solution)/shard_map/near_1/pallas_call | solution.py:119
  153.7 3.6 %kv_1.1.refs_8_.refs_0_.refs_1_ = bf16[256,512]{1,0:T(8,128)(2,1)} custom-call(s32[1]{0:T(128)} %bitcast.3.order_ref, bf16[128,2048]{1,0:T(8,128)(2,1)} %copy-done.1, bf16[128,2048]{1,0:T(8,128)(2,1)} %collective-permute-done.11.refs_1_, f32[4,1,2048]{2,1,0:T(1,128)} %bitcast.18, bf16[8192,512]{1,0:T(8,128)(2,1)} %refs_3_.12, ...), custom_call_target="tpu_custom_call" | custom-call | flops 1000 | bytes 1000 | tf_op jit(solution)/shard_map/kv_1/pallas_call | solution.py:173
  157.8 2.2 collective-permute-start.14
  160.0 7.9 %query_1.1.refs_4_.q_ref.refs_1_ = bf16[256,2048]{1,0:T(8,128)(2,1)} custom-call(s32[1]{0:T(128)} %bitcast.3.order_ref, bf16[128,2048]{1,0:T(8,128)(2,1)} %copy-done.1, bf16[128,2048]{1,0:T(8,128)(2,1)} %collective-permute-done.11.refs_1_, f32[4,1,2048]{2,1,0:T(1,128)} %bitcast.19, bf16[8192,2048]{1,0:T(8,128)(2,1)} %refs_3_.13, ...), custom_call_target="tpu_custom_call" | custom-call | flops 1000 | bytes 1000 | tf_op jit(solution)/shard_map/query_1/pallas_call | solution.py:173
  169.4 2.2 pack_1.1.refs_4_
  171.6 13.8 %collective-permute-start.15 = (bf16[1024,512]{1,0:T(8,128)(2,1)}, bf16[1024,512]{1,0:T(8,128)(2,1)}, u32[]{:S(2)}, u32[]{:S(2)}) collective-permute-start(bf16[1024,512]{1,0:T(8,128)(2,1)} %pack_1.1.refs_4_), channel_id=1, source_target_pairs={{0,4},{4,0},{8,12},{12,8},{16,20},{20,16},{24,28},{28,24},{1,5},{5... | collective-permute-start | bytes 3145736 | tf_op jit(solution)/shard_map/ppermute | solution.py:27
  185.4 19.6 %early_1.1.refs_3_ = f32[2,144,2048]{2,1,0:T(8,128)} custom-call(s32[3]{0:T(128)} %pad_add_fusion.place_ref, bf16[256,2048]{1,0:T(8,128)(2,1)} %query_1.1.refs_4_.q_ref.refs_1_, bf16[256,512]{1,0:T(8,128)(2,1)} %kv_0.1.refs_8_.refs_0_, bf16[256,512]{1,0:T(8,128)(2,1)} %kv_1.1.refs_8_.refs_0_.refs_1_, ...), custom_call_target="tpu_custom_call" | custom-call | flops 1000 | bytes 1000 | tf_op jit(solution)/shard_map/early_1/pallas_call | solution.py:301
  205.0 28.3 %late_256.1 = (bf16[4,512,512]{2,1,0:T(8,128)(2,1)}, bf16[512,2048]{1,0:T(8,128)(2,1)}) custom-call(s32[3]{0:T(128)} %pad_add_fusion.place_ref, bf16[256,2048]{1,0:T(8,128)(2,1)} %query_0.1.refs_4_.q_ref.refs_0_, bf16[256,2048]{1,0:T(8,128)(2,1)} %query_1.1.refs_4_.q_ref.refs_1_, ...), custom_call_target="tpu_custom_call", output_to_operand_aliasing={{0}: (7, {})} | custom-call | flops 1000 | bytes 1000 | tf_op jit(solution)/shard_map/late_256/pallas_call | solution.py:445
  (52 shorter events, 20.8 us)
Async XLA Ops:
  2.8 24.4 %collective-permute-start = (bf16[256,2048]{1,0:T(8,128)(2,1)}, bf16[256,2048]{1,0:T(8,128)(2,1)}, u32[]{:S(2)}, u32[]{:S(2)}) collective-permute-start(bf16[256,2048]{1,0:T(8,128)(2,1)} %cut_0.1.refs_4_), channel_id=1, source_target_pairs={{0,1},{1,2},{2,3},{3,0},{4,5},{5,6},{6,7},{7,4},{8,9},{9,10},{10,1... | collective-permute-start | bytes 3145736 | tf_op jit(solution)/shard_map/ppermute | solution.py:23
  4.2 48.4 %collective-permute-start.2 = (bf16[256,2048]{1,0:T(8,128)(2,1)}, bf16[256,2048]{1,0:T(8,128)(2,1)}, u32[]{:S(2)}, u32[]{:S(2)}) collective-permute-start(bf16[256,2048]{1,0:T(8,128)(2,1)} %cut_0.1.refs_4_), channel_id=1, source_target_pairs={{0,3},{1,0},{2,1},{3,2},{4,7},{5,4},{6,5},{7,6},{8,11},{9,8},{10,9... | collective-permute-start | bytes 3145736 | tf_op jit(solution)/shard_map/ppermute | solution.py:23
  29.1 45.7 %collective-permute-start.1 = (bf16[128,2048]{1,0:T(8,128)(2,1)}, bf16[128,2048]{1,0:T(8,128)(2,1)S(1)}, u32[]{:S(2)}, u32[]{:S(2)}) collective-permute-start(bf16[128,2048]{1,0:T(8,128)(2,1)} %pass_0_1.1.refs_0_), channel_id=1, source_target_pairs={{0,1},{1,2},{2,3},{3,0},{4,5},{5,6},{6,7},{7,4},{8,9},{9,10},{10,1... | collective-permute-start | bytes 1572872 | tf_op jit(solution)/shard_map/ppermute | solution.py:23
  54.4 20.4 %collective-permute-start.3 = (bf16[128,2048]{1,0:T(8,128)(2,1)}, bf16[128,2048]{1,0:T(8,128)(2,1)}, u32[]{:S(2)}, u32[]{:S(2)}) collective-permute-start(bf16[128,2048]{1,0:T(8,128)(2,1)} %pass_0_2.1.refs_0_), channel_id=1, source_target_pairs={{0,3},{1,0},{2,1},{3,2},{4,7},{5,4},{6,5},{7,6},{8,11},{9,8},{10,9... | collective-permute-start | bytes 1572872 | tf_op jit(solution)/shard_map/ppermute | solution.py:23
  74.8 0.8 copy-start
  79.2 12.0 %collective-permute-start.5 = (bf16[256,512]{1,0:T(8,128)(2,1)}, bf16[256,512]{1,0:T(8,128)(2,1)S(1)}, u32[]{:S(2)}, u32[]{:S(2)}) collective-permute-start(bf16[256,512]{1,0:T(8,128)(2,1)} %kv_0.1.refs_8_.refs_0_), channel_id=1, source_target_pairs={{0,8},{4,12},{8,0},{12,4},{16,24},{20,28},{24,16},{28,20},{1,9},{5... | collective-permute-start | bytes 786440 | tf_op jit(solution)/shard_map/ppermute | solution.py:27
  79.5 11.8 %collective-permute-start.6 = (bf16[256,512]{1,0:T(8,128)(2,1)}, bf16[256,512]{1,0:T(8,128)(2,1)S(1)}, u32[]{:S(2)}, u32[]{:S(2)}) collective-permute-start(bf16[256,512]{1,0:T(8,128)(2,1)} %kv_0.1.refs_8_.refs_0_), channel_id=1, source_target_pairs={{0,16},{4,20},{8,24},{12,28},{16,0},{20,4},{24,8},{28,12},{1,17},{... | collective-permute-start | bytes 786440 | tf_op jit(solution)/shard_map/ppermute | solution.py:27
  79.5 12.3 %collective-permute-start.7 = (bf16[256,512]{1,0:T(8,128)(2,1)}, bf16[256,512]{1,0:T(8,128)(2,1)S(1)}, u32[]{:S(2)}, u32[]{:S(2)}) collective-permute-start(bf16[256,512]{1,0:T(8,128)(2,1)} %kv_0.1.refs_8_.refs_0_), channel_id=1, source_target_pairs={{0,24},{4,28},{8,16},{12,20},{16,8},{20,12},{24,0},{28,4},{1,25},{... | collective-permute-start | bytes 786440 | tf_op jit(solution)/shard_map/ppermute | solution.py:27
  81.9 23.9 %collective-permute-start.4 = (bf16[256,2048]{1,0:T(8,128)(2,1)}, bf16[256,2048]{1,0:T(8,128)(2,1)}, u32[]{:S(2)}, u32[]{:S(2)}) collective-permute-start(bf16[256,2048]{1,0:T(8,128)(2,1)} %cut_1.1.refs_17_), channel_id=1, source_target_pairs={{0,1},{1,2},{2,3},{3,0},{4,5},{5,6},{6,7},{7,4},{8,9},{9,10},{10,1... | collective-permute-start | bytes 3145736 | tf_op jit(solution)/shard_map/ppermute | solution.py:23
  91.2 6.9 %copy-start.8 = (s32[4]{0:T(128)S(1)}, s32[4]{0:T(128)}, u32[]{:S(2)}) copy-start(s32[4]{0:T(128)} %param.11) | copy-start | bytes 52
  91.2 0.7 copy-start.2
  91.2 0.8 copy-start.3
  92.0 0.7 copy-start.5
  94.9 13.9 %collective-permute-start.10 = (bf16[1024,512]{1,0:T(8,128)(2,1)}, bf16[1024,512]{1,0:T(8,128)(2,1)}, u32[]{:S(2)}, u32[]{:S(2)}) collective-permute-start(bf16[1024,512]{1,0:T(8,128)(2,1)} %pack_0.1.refs_1_.refs_2_), channel_id=1, source_target_pairs={{0,4},{4,0},{8,12},{12,8},{16,20},{20,16},{24,28},{28,24},{1,5},{5... | collective-permute-start | bytes 3145736 | tf_op jit(solution)/shard_map/ppermute | solution.py:27
  97.6 37.5 %collective-permute-start.9 = (bf16[256,2048]{1,0:T(8,128)(2,1)}, bf16[256,2048]{1,0:T(8,128)(2,1)}, u32[]{:S(2)}, u32[]{:S(2)}) collective-permute-start(bf16[256,2048]{1,0:T(8,128)(2,1)} %cut_1.1.refs_17_), channel_id=1, source_target_pairs={{0,3},{1,0},{2,1},{3,2},{4,7},{5,4},{6,5},{7,6},{8,11},{9,8},{10,9... | collective-permute-start | bytes 3145736 | tf_op jit(solution)/shard_map/ppermute | solution.py:23
  107.6 45.3 %collective-permute-start.8 = (bf16[128,2048]{1,0:T(8,128)(2,1)}, bf16[128,2048]{1,0:T(8,128)(2,1)S(1)}, u32[]{:S(2)}, u32[]{:S(2)}) collective-permute-start(bf16[128,2048]{1,0:T(8,128)(2,1)} %pass_1_1.1.refs_4_), channel_id=1, source_target_pairs={{0,1},{1,2},{2,3},{3,0},{4,5},{5,6},{6,7},{7,4},{8,9},{9,10},{10,1... | collective-permute-start | bytes 1572872 | tf_op jit(solution)/shard_map/ppermute | solution.py:23
  137.0 16.0 %collective-permute-start.11 = (bf16[128,2048]{1,0:T(8,128)(2,1)}, bf16[128,2048]{1,0:T(8,128)(2,1)}, u32[]{:S(2)}, u32[]{:S(2)}) collective-permute-start(bf16[128,2048]{1,0:T(8,128)(2,1)} %pass_1_2.1.refs_17_), channel_id=1, source_target_pairs={{0,3},{1,0},{2,1},{3,2},{4,7},{5,4},{6,5},{7,6},{8,11},{9,8},{10,9... | collective-permute-start | bytes 1572872 | tf_op jit(solution)/shard_map/ppermute | solution.py:23
  152.9 0.8 copy-start.1
  157.3 10.6 %collective-permute-start.12 = (bf16[256,512]{1,0:T(8,128)(2,1)}, bf16[256,512]{1,0:T(8,128)(2,1)S(1)}, u32[]{:S(2)}, u32[]{:S(2)}) collective-permute-start(bf16[256,512]{1,0:T(8,128)(2,1)} %kv_1.1.refs_8_.refs_0_.refs_1_), channel_id=1, source_target_pairs={{0,8},{4,12},{8,0},{12,4},{16,24},{20,28},{24,16},{28,20},{1,9},{5... | collective-permute-start | bytes 786440 | tf_op jit(solution)/shard_map/ppermute | solution.py:27
  157.6 10.3 %collective-permute-start.13 = (bf16[256,512]{1,0:T(8,128)(2,1)}, bf16[256,512]{1,0:T(8,128)(2,1)S(1)}, u32[]{:S(2)}, u32[]{:S(2)}) collective-permute-start(bf16[256,512]{1,0:T(8,128)(2,1)} %kv_1.1.refs_8_.refs_0_.refs_1_), channel_id=1, source_target_pairs={{0,16},{4,20},{8,24},{12,28},{16,0},{20,4},{24,8},{28,12},{1,17},{... | collective-permute-start | bytes 786440 | tf_op jit(solution)/shard_map/ppermute | solution.py:27
  157.8 10.1 %collective-permute-start.14 = (bf16[256,512]{1,0:T(8,128)(2,1)}, bf16[256,512]{1,0:T(8,128)(2,1)S(1)}, u32[]{:S(2)}, u32[]{:S(2)}) collective-permute-start(bf16[256,512]{1,0:T(8,128)(2,1)} %kv_1.1.refs_8_.refs_0_.refs_1_), channel_id=1, source_target_pairs={{0,24},{4,28},{8,16},{12,20},{16,8},{20,12},{24,0},{28,4},{1,25},{... | collective-permute-start | bytes 786440 | tf_op jit(solution)/shard_map/ppermute | solution.py:27
  167.9 0.7 copy-start.4
  167.9 0.8 copy-start.6
  171.6 33.4 %collective-permute-start.15 = (bf16[1024,512]{1,0:T(8,128)(2,1)}, bf16[1024,512]{1,0:T(8,128)(2,1)}, u32[]{:S(2)}, u32[]{:S(2)}) collective-permute-start(bf16[1024,512]{1,0:T(8,128)(2,1)} %pack_1.1.refs_4_), channel_id=1, source_target_pairs={{0,4},{4,0},{8,12},{12,8},{16,20},{20,16},{24,28},{28,24},{1,5},{5... | collective-permute-start | bytes 3145736 | tf_op jit(solution)/shard_map/ppermute | solution.py:27
  (1 other events, 0.7 us)
